TPU v7x, 256 devices: a whole 4x4x8 slice. The times are simulated.
256 devices in a mesh: row: 64 (over z, y, x_hi), col: 4 (over x_lo, core).
Axes of the slice: x: 4 (x_hi: 2, x_lo: 2; x = x_hi * 2 + x_lo), y: 4, z: 8, core: 2. Of those that a mesh axis runs over, the one named last changes fastest.
Arguments:
- pair_rep: float32 [384, 384, 128], P('row', 'col'), may hold values from -6 to 6
- proj_weights: bfloat16 [2, 4, 128, 128], replicated, may hold values from -0.5 to 0.5
- gate_weights: bfloat16 [2, 128, 128], replicated, may hold values from -0.5 to 0.5
- out_weights: bfloat16 [2, 128, 128], replicated, may hold values from -0.5 to 0.5
Outputs:
- pair_out: float32 [384, 384, 128], P('row', 'col')
All inputs are finite; a program needn't handle non-finite values.
Results may differ from a plain program's by a relative error of at most 0.013.
Values may be sent and summed in bfloat16 or wider, within the bound.
A program may use at most 128 MiB of HBM per device.

v0:
```python
import jax
import jax.numpy as jnp
from jax import lax
from jax.sharding import PartitionSpec as P


def normed(values):
    centred = values - jnp.mean(values, axis=-1, keepdims=True)
    variance = jnp.mean(centred * centred, axis=-1, keepdims=True)
    return centred * lax.rsqrt(variance + 1e-05)


def outgoing_product(left_edge, right_edge):
    partial_sums = jnp.einsum(
        "ikc,jkc->ijc",
        left_edge,
        lax.all_gather(right_edge, "row", axis=0, tiled=True),
        preferred_element_type=jnp.float32,
    )
    return lax.psum_scatter(
        partial_sums.astype(jnp.bfloat16), "col", scatter_dimension=1, tiled=True
    ).astype(jnp.float32)


def incoming_product(left_edge, right_edge):
    left_rows = lax.all_gather(left_edge, "col", axis=1, tiled=True)
    return lax.psum_scatter(
        jnp.einsum("kic,kjc->ijc", left_rows, right_edge, preferred_element_type=jnp.float32),
        "row",
        scatter_dimension=0,
        tiled=True,
    )


def update(pair_block, proj_weights, gate_weights, out_weights, layer_index, outgoing):
    side_a, side_b, channels = pair_block.shape
    flat_norm = normed(pair_block).astype(jnp.bfloat16).reshape(side_a * side_b, channels)

    def linear(matrix):
        return jnp.dot(flat_norm, matrix, preferred_element_type=jnp.float32).reshape(
            side_a, side_b, matrix.shape[1]
        )

    left_edge = (
        jax.nn.sigmoid(linear(proj_weights[layer_index, 0])) * linear(proj_weights[layer_index, 1])
    ).astype(jnp.bfloat16)
    right_edge = (
        jax.nn.sigmoid(linear(proj_weights[layer_index, 2])) * linear(proj_weights[layer_index, 3])
    ).astype(jnp.bfloat16)
    if outgoing:
        triangle = outgoing_product(left_edge, right_edge)
    else:
        triangle = incoming_product(left_edge, right_edge)
    tri_norm = normed(triangle).astype(jnp.bfloat16).reshape(side_a * side_b, -1)
    projected = jnp.dot(
        tri_norm, out_weights[layer_index], preferred_element_type=jnp.float32
    ).reshape(side_a, side_b, channels)
    return pair_block + jax.nn.sigmoid(linear(gate_weights[layer_index])) * projected


def per_device(pair_rep, proj_weights, gate_weights, out_weights):
    first = update(pair_rep, proj_weights, gate_weights, out_weights, 0, True)
    return update(first, proj_weights, gate_weights, out_weights, 1, False)


def solution(mesh):
    return jax.shard_map(
        per_device,
        mesh=mesh,
        in_specs=(P("row", "col", None), P(), P(), P()),
        out_specs=P("row", "col", None),
        check_vma=False,
    )
```

profile of v0, /device:TPU:1, one launch (start us, length us, event | category | flops | bytes accessed | tf_op | source)
XLA Modules:
  0.0 1144.2 jit_solution(12458466556901255226)
XLA Ops:
  6.5 0.0 all-gather.2.cloned.1.call-start
  6.5 1.1 reduce_sum.72
  7.7 1.3 multiply_reduce_fusion.2
  9.0 1.2 multiply_convert_fusion.2
  10.1 1.0 fusion.17
  11.1 1.6 fusion.21
  12.7 0.0 all-gather.2.cloned.1.call-update
  12.8 0.0 reduce-scatter.3.cloned.1.call-start
  12.8 1.0 fusion.14
  13.8 0.9 fusion.22
  14.7 0.2 copy.42
  14.9 157.6 %all-gather.2.cloned.1.call-done = bf16[384,96,128]{2,1,0:T(8,128)(2,1)} async-done(((bf16[6,96,128]{2,1,0:T(8,128)(2,1)}), bf16[384,96,128]{2,1,0:T(8,128)(2,1)}) %all-gather.2.cloned.1.call-update) | async-done | bytes 9437200 | tf_op jit(solution)/shard_map/all_gather | solution.py:17
  172.6 15.6 %copy.41 = bf16[384,96,128]{1,0,2:T(8,128)(2,1)} copy(bf16[384,96,128]{2,1,0:T(8,128)(2,1)} %all-gather.2.cloned.1.call-done) | data formatting | bytes 18874368 | tf_op jit(solution)/shard_map/all_gather | solution.py:17
  188.1 0.0 copy-start.3
  188.1 0.0 copy-start
  188.1 0.0 copy-start.2
  188.1 0.0 copy-start.1
  188.1 9.1 fusion
  197.2 1.6 copy.43
  198.8 0.0 reduce-scatter.3.cloned.1.call-update
  198.8 0.0 reduce-scatter.5.cloned.1.call-start
  198.9 0.0 copy-done.3
  198.9 0.2 fusion.20
  199.1 20.0 %reduce-scatter.3.cloned.1.call-done = bf16[6,96,128]{2,0,1:T(8,128)(2,1)} async-done(((bf16[6,384,128]{2,0,1:T(8,128)(2,1)}), bf16[6,96,128]{2,0,1:T(8,128)(2,1)}) %reduce-scatter.3.cloned.1.call-update) | async-done | bytes 147472 | tf_op jit(solution)/shard_map/reduce_scatter | solution.py:20
  219.1 1.1 convert_reduce_fusion
  220.2 0.1 copy.44
  220.2 0.1 copy.45
  220.4 1.2 fusion.27
  221.6 0.1 copy.46
  221.7 0.1 copy.47
  221.8 1.2 fusion.28
  223.0 0.0 copy-done
  223.0 0.0 copy-done.2
  223.0 0.3 fusion.56
  223.4 0.3 multiply_reduce_fusion.1
  223.7 0.2 multiply_convert_fusion.1
  223.9 0.0 copy-done.1
  223.9 0.2 fusion.5
  224.1 0.2 fusion.8
  224.4 0.2 fusion.24
  224.5 7.7 all_gather.7
  232.2 0.5 copy.50
  232.7 0.2 fusion.23
  232.9 0.2 copy.49
  233.1 7.9 convolution_bitcast_fusion
  241.0 19.0 %copy.51 = f32[384,96,128]{2,1,0:T(8,128)} copy(f32[384,96,128]{0,1,2:T(8,128)} %convolution_bitcast_fusion) | data formatting | bytes 37748736 | tf_op jit(solution)/shard_map/kic,kjc->ijc/transpose | solution.py:28
  260.0 0.0 reduce-scatter.5.cloned.1.call-update
  260.1 0.2 fusion.11
  260.3 872.9 %reduce-scatter.5.cloned.1.call-done = f32[6,96,128]{2,1,0:T(8,128)} async-done(((f32[384,96,128]{2,1,0:T(8,128)}), f32[6,96,128]{2,1,0:T(8,128)}) %reduce-scatter.5.cloned.1.call-update) | async-done | bytes 294928 | tf_op jit(solution)/shard_map/reduce_scatter | solution.py:27
  1133.2 1.1 reduce_sum.78
  1134.3 1.3 multiply_reduce_fusion
  1135.6 2.0 fusion.1
  (8 shorter events, 0.0 us)
Async XLA Ops:
  6.5 166.0 %all-gather.2.cloned.1.call-start = ((), (), s32[]{:S(2)}) async-start(), calls=%async_computation.2 | async-start | bytes 9584640 | tf_op jit(solution)/shard_map/all_gather | solution.py:17
  12.8 206.3 %reduce-scatter.3.cloned.1.call-start = ((), (), s32[]{:S(2)}) async-start(), calls=%async_computation.3 | async-start | bytes 983040 | tf_op jit(solution)/shard_map/reduce_scatter | solution.py:20
  188.1 10.7 copy-start.3
  188.1 34.9 %copy-start = (f32[6,96,128]{2,1,0:T(8,128)S(1)}, f32[6,96,128]{2,1,0:T(8,128)}, u32[]{:S(2)}) copy-start(f32[6,96,128]{2,1,0:T(8,128)} %param.4) | copy-start | bytes 884740
  188.1 34.9 %copy-start.2 = (bf16[2,128,128]{2,1,0:T(8,128)(2,1)S(1)}, bf16[2,128,128]{2,1,0:T(8,128)(2,1)}, u32[]{:S(2)}) copy-start(bf16[2,128,128]{2,1,0:T(8,128)(2,1)} %param.7) | copy-start | bytes 196612
  188.1 35.8 %copy-start.1 = (bf16[2,4,128,128]{3,2,1,0:T(8,128)(2,1)S(1)}, bf16[2,4,128,128]{3,2,1,0:T(8,128)(2,1)}, u32[]{:S(2)}) copy-start(bf16[2,4,128,128]{3,2,1,0:T(8,128)(2,1)} %param.5) | copy-start | bytes 786436
  198.8 934.4 %reduce-scatter.5.cloned.1.call-start = ((), (), s32[]{:S(2)}) async-start(), calls=%async_computation.4 | async-start | bytes 19169280 | tf_op jit(solution)/shard_map/reduce_scatter | solution.py:27
Sparse Core Ops, SparseCore 0:
  12.9 159.6 all-gather.1
  198.9 20.0 reduce-scatter.2
  260.2 872.9 reduce-scatter.4
where the time goes:
time: 1150 us; the launch traced here: 1140 us
  waiting for transfers between devices  1050 us (91%)
  local copies, waits for them, and re-layouts  37.4 us (3%)
  matrix products  25.1 us (2%)
  between operations  13.3 us (1%)
    reduce_scatter x1, waiting for transfers between devices, incoming_product(): lax.psum_scatter(jnp.einsum('kic,kjc->ijc', left_rows, right_edge, prefer...  873 us
    all_gather x1, waiting for transfers between devices, outgoing_product(): lax.all_gather(right_edge, 'row', axis=0, tiled=True)  158 us
  transfers between devices with their start and end apart: 3, of which 3 were waited for; matrix products, arithmetic and copies ran while one was open for 0% of the time, Pallas kernels for 0%

commit v1 on v0

v1 whole, which is shorter than its diff:
```python
import jax
import jax.numpy as jnp
from jax import lax
from jax.sharding import PartitionSpec as P


def normed(values):
    centred = values - jnp.mean(values, axis=-1, keepdims=True)
    variance = jnp.mean(centred * centred, axis=-1, keepdims=True)
    return centred * lax.rsqrt(variance + 1e-05)


def triangle(left_edge, right_edge, outgoing, rows):
    a, b, channels = left_edge.shape
    per = channels // rows
    edges = jnp.stack([left_edge, right_edge]).transpose(3, 0, 1, 2).reshape(rows, per, 2, a, b)
    edges = lax.all_to_all(edges, "row", split_axis=0, concat_axis=0, tiled=True)
    edges = edges.transpose(1, 2, 0, 3, 4).reshape(per, 2, rows * a, b)
    left, right = edges[:, 0], edges[:, 1]
    if outgoing:
        left = lax.all_gather(left, "col", axis=2, tiled=True)
        right = lax.all_to_all(right, "col", split_axis=1, concat_axis=2, tiled=True)
        tri = jnp.einsum("cik,cjk->cij", left, right, preferred_element_type=jnp.float32)
    else:
        left = lax.all_gather(left, "col", axis=2, tiled=True)
        tri = jnp.einsum("cki,ckj->cij", left, right, preferred_element_type=jnp.float32)
    tri = tri.astype(jnp.bfloat16).reshape(per, rows, a, b).transpose(1, 0, 2, 3)
    tri = lax.all_to_all(tri, "row", split_axis=0, concat_axis=0, tiled=True)
    return tri.reshape(channels, a, b).transpose(1, 2, 0).astype(jnp.float32)


def update(pair_block, proj_weights, gate_weights, out_weights, layer_index, outgoing, rows):
    side_a, side_b, channels = pair_block.shape
    flat_norm = normed(pair_block).astype(jnp.bfloat16).reshape(side_a * side_b, channels)

    def linear(matrix):
        return jnp.dot(flat_norm, matrix, preferred_element_type=jnp.float32).reshape(
            side_a, side_b, matrix.shape[1]
        )

    left_edge = (
        jax.nn.sigmoid(linear(proj_weights[layer_index, 0])) * linear(proj_weights[layer_index, 1])
    ).astype(jnp.bfloat16)
    right_edge = (
        jax.nn.sigmoid(linear(proj_weights[layer_index, 2])) * linear(proj_weights[layer_index, 3])
    ).astype(jnp.bfloat16)
    tri = triangle(left_edge, right_edge, outgoing, rows)
    tri_norm = normed(tri).astype(jnp.bfloat16).reshape(side_a * side_b, -1)
    projected = jnp.dot(
        tri_norm, out_weights[layer_index], preferred_element_type=jnp.float32
    ).reshape(side_a, side_b, channels)
    return pair_block + jax.nn.sigmoid(linear(gate_weights[layer_index])) * projected


def solution(mesh):
    rows = mesh.shape["row"]

    def per_device(pair_rep, proj_weights, gate_weights, out_weights):
        first = update(pair_rep, proj_weights, gate_weights, out_weights, 0, True, rows)
        return update(first, proj_weights, gate_weights, out_weights, 1, False, rows)

    return jax.shard_map(
        per_device,
        mesh=mesh,
        in_specs=(P("row", "col", None), P(), P(), P()),
        out_specs=P("row", "col", None),
        check_vma=False,
    )
```

time: 1150 us -> 128 us (0.11)
  waiting for transfers between devices: 1050 us -> 23.1 us
  blocking collectives: 7.67 us -> 68.2 us
  local copies, waits for them, and re-layouts: 37.4 us -> 11.5 us
  matrix products: 25.1 us -> 3.94 us
  starting transfers between devices: 0.09 us -> 17.6 us
  between operations: 13.3 us -> 0.43 us
    reduce_scatter x2 -> x0, waiting for transfers between devices: 893 us -> none  [the longest x1 873 us: incoming_product(): lax.psum_scatter(jnp.einsum('kic,kjc->ijc', left_rows, right_edge, prefer...]
    all_gather x1 -> x0, waiting for transfers between devices: 158 us -> none  [outgoing_product(): lax.all_gather(right_edge, 'row', axis=0, tiled=True)]
    all_to_all x0 -> x2, blocking collectives: none -> 48.5 us  [triangle(): lax.all_to_all(edges, 'row', split_axis=0, concat_axis=0, tiled=True)]
    all_to_all x0 -> x3, waiting for transfers between devices: none -> 23.1 us  [the longest x2 23.1 us: triangle(): tri = lax.all_to_all(tri, 'row', split_axis=0, concat_axis=0, tiled=True)]
    transpose x1 -> x4, local copies, waits for them, and re-layouts: 19 us -> 1.07 us  [the longest x2 0.61 us: triangle(): edges = edges.transpose(1, 2, 0, 3, 4).reshape(per, 2, rows * a, b)]
    all_to_all x0 -> x3, starting transfers between devices: none -> 17.6 us  [the longest x2 11.3 us: triangle(): tri = lax.all_to_all(tri, 'row', split_axis=0, concat_axis=0, tiled=True)]
    dot_general x2, matrix products: 17 us -> 0.58 us  [the longest x1 0.32 us: triangle(): jnp.einsum('cik,cjk->cij', left, right, preferred_element_type=jnp.float32)]
    all_gather x2, local copies, waits for them, and re-layouts: 16.1 us -> 1.98 us  [triangle(): left = lax.all_gather(left, 'col', axis=2, tiled=True)]
  transfers between devices with their start and end apart: 3 -> 3, of which waited for: 3 -> 2; matrix products, arithmetic and copies ran while one was open for 0% -> 1% of each run, Pallas kernels for 0% -> 0%
where the time goes in v1:
time: 128 us; the launch traced here: 127 us
  blocking collectives  68.2 us (53%)
  waiting for transfers between devices  23.1 us (18%)
  starting transfers between devices  17.6 us (14%)
  local copies, waits for them, and re-layouts  11.5 us (9%)
  matrix products  3.94 us (3%)
  other arithmetic  2.58 us (2%)
    all_to_all x2, blocking collectives, triangle(): lax.all_to_all(edges, 'row', split_axis=0, concat_axis=0, tiled=True)  48.5 us
    all_to_all x2, waiting for transfers between devices, triangle(): tri = lax.all_to_all(tri, 'row', split_axis=0, concat_axis=0, tiled=True)  23.1 us
    all_gather x2, blocking collectives, triangle(): left = lax.all_gather(left, 'col', axis=2, tiled=True)  19.7 us
    all_to_all x2, starting transfers between devices, triangle(): tri = lax.all_to_all(tri, 'row', split_axis=0, concat_axis=0, tiled=True)  11.3 us
    all_to_all x1, starting transfers between devices, triangle(): lax.all_to_all(right, 'col', split_axis=1, concat_axis=2, tiled=True)  6.33 us
    slice x5, local copies, waits for them, and re-layouts, triangle(): left, right = (edges[:, 0], edges[:, 1])  2.6 us
  transfers between devices with their start and end apart: 3, of which 2 were waited for; matrix products, arithmetic and copies ran while one was open for 1% of the time, Pallas kernels for 0%

profile of v1, /device:TPU:1, one launch (start us, length us, event | category | flops | bytes accessed | tf_op | source)
XLA Modules:
  0.0 127.3 jit_solution(11006790090724109200)
XLA Ops:
  0.0 0.0 copy-start
  0.0 1.2 reduce_sum.72
  1.2 0.0 copy-done
  1.2 0.3 multiply_reduce_fusion.3
  1.5 0.0 copy-start.1
  1.6 0.2 multiply_convert_fusion.3
  1.8 0.7 copy-done.1
  2.5 0.2 fusion.13
  2.7 0.2 fusion.16
  2.9 0.2 fusion.26
  3.1 0.2 fusion.27
  3.4 0.2 copy.106
  3.6 0.3 copy.107
  3.9 29.3 %all_to_all.38 = bf16[64,2,2,6,96]{4,1,3,2,0:T(2,128)(2,1)S(1)} all-to-all(bf16[64,2,2,6,96]{4,1,3,2,0:T(2,128)(2,1)S(1)} %copy.107), channel_id=1, replica_groups=mesh['row'=64,'col'=4] {'row'}, dimensions={0} | all-to-all | bytes 589824 | tf_op jit(solution)/shard_map/all_to_all | solution.py:17
  33.1 0.3 copy.108
  33.4 0.5 fusion.60
  34.0 0.6 copy.109
  34.6 0.3 copy.111
  34.9 0.9 copy.112
  35.8 6.3 %all-to-all-start.1 = ((bf16[2,384,96]{2,0,1:T(2,128)(2,1)}), bf16[2,384,96]{2,0,1:T(2,128)(2,1)S(1)}, u32[]{:S(2)}, u32[]{:S(2)}) async-start(bf16[2,384,96]{2,0,1:T(2,128)(2,1)} %copy.112), calls=%async_computation.1 | async-start | bytes 393216 | tf_op jit(solution)/shard_map/all_to_all | solution.py:22
  42.1 9.2 %all-gather = bf16[2,1,384,384]{2,0,1,3:T(2,128)(2,1)S(1)} all-gather(bf16[2,1,384,96]{2,0,1,3:T(2,128)(2,1)S(1)} %copy.109), channel_id=2, replica_groups=mesh['row'=64,'col'=4] {'col'}, dimensions={3}, use_global_device_ids=true | all-gather | bytes 737280 | tf_op jit(solution)/shard_map/all_gather | solution.py:21
  51.3 1.0 copy.110
  52.3 0.0 all-to-all-done.1
  52.3 0.2 copy.134
  52.5 0.2 all_to_all.29
  52.7 0.3 convolution_convert_fusion.1
  53.0 0.9 copy.114
  53.8 0.0 copy-start.3
  53.8 5.7 %all-to-all-start.2 = ((bf16[64,2,6,96]{3,1,2,0:T(2,128)(2,1)}), bf16[64,2,6,96]{3,1,2,0:T(2,128)(2,1)S(1)}, u32[]{:S(2)}, u32[]{:S(2)}) async-start(bf16[64,2,6,96]{3,1,2,0:T(2,128)(2,1)} %bitcast.21), calls=%async_computation.2 | async-start | bytes 393216 | tf_op jit(solution)/shard_map/all_to_all | solution.py:28
  59.5 0.0 copy-done.3
  59.5 0.2 fusion.19
  59.8 11.5 %all-to-all-done.2 = bf16[64,2,6,96]{3,1,2,0:T(2,128)(2,1)S(1)} async-done(((bf16[64,2,6,96]{3,1,2,0:T(2,128)(2,1)}), bf16[64,2,6,96]{3,1,2,0:T(2,128)(2,1)S(1)}, u32[]{:S(2)}, u32[]{:S(2)}) %all-to-all-start.2) | async-done | bytes 147488 | tf_op jit(solution)/shard_map/all_to_all | solution.py:28
  71.3 0.3 copy.116
  71.7 0.0 copy-start.2
  71.7 0.1 multiply_reduce_fusion.1
  71.8 0.7 copy-done.2
  72.5 0.4 fusion.61
  72.9 0.3 multiply_reduce_fusion.2
  73.2 0.2 multiply_convert_fusion.2
  73.4 0.2 fusion.4
  73.7 0.2 fusion.7
  73.9 0.2 fusion.24
  74.1 0.2 fusion.25
  74.3 0.2 copy.118
  74.5 0.3 copy.119
  74.8 19.2 %all_to_all.39 = bf16[64,2,2,6,96]{4,1,3,2,0:T(2,128)(2,1)S(1)} all-to-all(bf16[64,2,2,6,96]{4,1,3,2,0:T(2,128)(2,1)S(1)} %copy.119), channel_id=1, replica_groups=mesh['row'=64,'col'=4] {'row'}, dimensions={0} | all-to-all | bytes 589824 | tf_op jit(solution)/shard_map/all_to_all | solution.py:17
  94.1 0.3 copy.120
  94.4 0.5 fusion.59
  94.9 0.3 copy.130
  95.3 0.6 copy.121
  95.9 10.5 %all-gather.1 = bf16[2,1,384,384]{2,0,1,3:T(2,128)(2,1)S(1)} all-gather(bf16[2,1,384,96]{2,0,1,3:T(2,128)(2,1)S(1)} %copy.121), channel_id=3, replica_groups=mesh['row'=64,'col'=4] {'col'}, dimensions={3}, use_global_device_ids=true | all-gather | bytes 737280 | tf_op jit(solution)/shard_map/all_gather | solution.py:25
  106.3 1.0 copy.122
  107.3 0.3 convolution_convert_fusion
  107.6 0.9 copy.124
  108.5 5.6 %all-to-all-start.4 = ((bf16[64,2,6,96]{3,1,2,0:T(2,128)(2,1)}), bf16[64,2,6,96]{3,1,2,0:T(2,128)(2,1)S(1)}, u32[]{:S(2)}, u32[]{:S(2)}) async-start(bf16[64,2,6,96]{3,1,2,0:T(2,128)(2,1)} %bitcast.46), calls=%async_computation.4 | async-start | bytes 393216 | tf_op jit(solution)/shard_map/all_to_all | solution.py:28
  114.0 0.2 fusion.10
  114.3 11.5 %all-to-all-done.4 = bf16[64,2,6,96]{3,1,2,0:T(2,128)(2,1)S(1)} async-done(((bf16[64,2,6,96]{3,1,2,0:T(2,128)(2,1)}), bf16[64,2,6,96]{3,1,2,0:T(2,128)(2,1)S(1)}, u32[]{:S(2)}, u32[]{:S(2)}) %all-to-all-start.4) | async-done | bytes 147488 | tf_op jit(solution)/shard_map/all_to_all | solution.py:28
  125.8 0.3 copy.126
  126.2 0.1 multiply_reduce_fusion
  126.3 1.0 fusion
  (14 shorter events, 0.2 us)
Async XLA Ops:
  0.0 1.2 copy-start
  1.5 1.0 copy-start.1
  35.8 16.5 %all-to-all-start.1 = ((bf16[2,384,96]{2,0,1:T(2,128)(2,1)}), bf16[2,384,96]{2,0,1:T(2,128)(2,1)S(1)}, u32[]{:S(2)}, u32[]{:S(2)}) async-start(bf16[2,384,96]{2,0,1:T(2,128)(2,1)} %copy.112), calls=%async_computation.1 | async-start | bytes 393216 | tf_op jit(solution)/shard_map/all_to_all | solution.py:22
  53.8 5.7 %copy-start.3 = (bf16[2,128,128]{2,1,0:T(8,128)(2,1)S(1)}, bf16[2,128,128]{2,1,0:T(8,128)(2,1)}, u32[]{:S(2)}) copy-start(bf16[2,128,128]{2,1,0:T(8,128)(2,1)} %param.6) | copy-start | bytes 196612
  53.8 17.4 %all-to-all-start.2 = ((bf16[64,2,6,96]{3,1,2,0:T(2,128)(2,1)}), bf16[64,2,6,96]{3,1,2,0:T(2,128)(2,1)S(1)}, u32[]{:S(2)}, u32[]{:S(2)}) async-start(bf16[64,2,6,96]{3,1,2,0:T(2,128)(2,1)} %bitcast.21), calls=%async_computation.2 | async-start | bytes 393216 | tf_op jit(solution)/shard_map/all_to_all | solution.py:28
  71.7 0.8 copy-start.2
  108.5 17.4 %all-to-all-start.4 = ((bf16[64,2,6,96]{3,1,2,0:T(2,128)(2,1)}), bf16[64,2,6,96]{3,1,2,0:T(2,128)(2,1)S(1)}, u32[]{:S(2)}, u32[]{:S(2)}) async-start(bf16[64,2,6,96]{3,1,2,0:T(2,128)(2,1)} %bitcast.46), calls=%async_computation.4 | async-start | bytes 393216 | tf_op jit(solution)/shard_map/all_to_all | solution.py:28

commit v2 on v1

v2 whole, which is shorter than its diff:
```python
import jax
import jax.numpy as jnp
from jax import lax
from jax.experimental import pallas as pl
from jax.experimental.pallas import tpu as pltpu
from jax.sharding import PartitionSpec as P

MESH = pl.DeviceIdType.MESH
F32, BF16 = jnp.float32, jnp.bfloat16
Z, CHIPS, YX, XLO, CORES = 8, 16, 8, 2, 2
A, B, C = 6, 96, 128
GROUP = C // Z
POS, LANES = A * B, 640
ROWS = Z * A
NT = (((1,), (1,)), ((), ()))
TN = (((0,), (0,)), ((), ()))


def normed(values, axis):
    centred = values - jnp.mean(values, axis=axis, keepdims=True)
    variance = jnp.mean(centred * centred, axis=axis, keepdims=True)
    return centred * lax.rsqrt(variance + 1e-05)


def dot(a, b, dims=(((1,), (0,)), ((), ()))):
    return lax.dot_general(a, b, dims, preferred_element_type=F32)


def lane_of(rows):
    return lax.broadcasted_iota(jnp.int32, (rows, 128), 1)


def split_rows(tiles):
    lane = lane_of(tiles[0].shape[0])
    t0, t1, t2, t3, t4 = tiles
    pieces = [
        t0,
        pltpu.roll(jnp.where(lane < 64, t1, t0), 32, 1),
        pltpu.roll(jnp.where(lane < 32, t2, t1), 64, 1),
        pltpu.roll(t2, 96, 1),
        t3,
        pltpu.roll(jnp.where(lane < 64, t4, t3), 32, 1),
    ]
    return [jnp.where(lane < B, piece, 0.0) for piece in pieces]


def join_rows(pieces):
    lane = lane_of(pieces[0].shape[0])
    r0, r1, r2, r3, r4, r5 = pieces
    r1, r2, r3, r5 = (pltpu.roll(r, s, 1) for r, s in ((r1, 96), (r2, 64), (r3, 32), (r5, 96)))
    return [
        jnp.where(lane < 96, r0, r1),
        jnp.where(lane < 64, r1, r2),
        jnp.where(lane < 32, r2, r3),
        jnp.where(lane < 96, r4, r5),
        r5,
    ]


def picks_outgoing(core):
    row = lax.broadcasted_iota(jnp.int32, (XLO * 128, YX * ROWS), 0)
    col = lax.broadcasted_iota(jnp.int32, (XLO * 128, YX * ROWS), 1)
    x_lo, jr = row // 128, row % 128
    z = 4 * x_lo + 2 * core + jr // 48
    source = (jr % 48) // A * ROWS + z * A + jr % A
    return jnp.where((col == source) & (jr < B), 1.0, 0.0).astype(BF16)


def picks_incoming(core):
    row = lax.broadcasted_iota(jnp.int32, (YX * ROWS, 4 * 128), 0)
    col = lax.broadcasted_iota(jnp.int32, (YX * ROWS, 4 * 128), 1)
    yx, z, r = row // ROWS, row % ROWS // A, row % A
    other = jnp.bitwise_xor((z // 2) % 2, core)
    source = (other * 2 + z // 4) * 128 + (z % 2) * 48 + yx * A + r
    return jnp.where(col == source, 1.0, 0.0).astype(BF16)


def kernel(
    z_ref, proj_ref, gate_ref, out_ref, o_ref,
    sendz, recvz, spread, sendp, recvp, sendq, recvq, gather, sendx, recvx,
    zs, zr, ps, pr, cs, cr, qs, qr, xs, xr,
):
    row, col = lax.axis_index("row"), lax.axis_index("col")
    plane, yx, x_lo, core = row // YX, row % YX, col // CORES, col % CORES
    chip = yx * XLO + x_lo

    def on_plane(other_plane):
        return {"row": other_plane * YX + yx, "col": col}

    def on_chip(other_chip):
        return {"row": plane * YX + other_chip // XLO, "col": other_chip % XLO * CORES + core}

    other_core = {"row": row, "col": x_lo * CORES + 1 - core}

    barrier = pltpu.get_barrier_semaphore()
    peers = [on_plane((plane + s) % Z) for s in range(1, Z)]
    peers += [on_chip((chip + s) % CHIPS) for s in range(1, CHIPS)] + [other_core]
    for peer in peers:
        pl.semaphore_signal(barrier, inc=1, device_id=peer, device_id_type=MESH)

    def remote(src, dst, send, recv, peer):
        pltpu.make_async_remote_copy(
            src_ref=src, dst_ref=dst, send_sem=send, recv_sem=recv, device_id=peer, device_id_type=MESH
        ).start()

    def arrived(ref, sem):
        pltpu.make_async_copy(ref, ref, sem).wait()

    def slot_of(some_chip):
        return some_chip % XLO * YX + some_chip // XLO

    def over_planes(src, dst, send, recv):
        for s in range(1, Z):
            peer = (plane + s) % Z
            remote(src.at[peer], dst.at[plane], send, recv, on_plane(peer))
        pltpu.make_async_copy(src.at[plane], dst.at[plane], recv).start()

    def over_chips(src, dst, send, recv):
        for s in range(1, CHIPS):
            peer = (chip + s) % CHIPS
            remote(src.at[slot_of(peer)], dst.at[slot_of(chip)], send, recv, on_chip(peer))
        pltpu.make_async_copy(src.at[slot_of(chip)], dst.at[slot_of(chip)], recv).start()

    pair = z_ref[...].reshape(POS, C)
    for u in range(2):
        zn = normed(pair, -1).astype(BF16)
        for side in range(2):
            gated = dot(proj_ref[u, 2 * side].astype(F32).T.astype(BF16), zn, NT)
            value = dot(proj_ref[u, 2 * side + 1].astype(F32).T.astype(BF16), zn, NT)
            edge = (jax.nn.sigmoid(gated) * value).astype(BF16)
            sendz[u, side, :, :, 0:POS] = edge.reshape(Z, GROUP, POS)
            if u == 0 and side == 0:
                pl.semaphore_wait(barrier, len(peers))
            over_planes(sendz.at[u, side], recvz.at[u, side], zs.at[u, side], zr.at[u, side])
        gate = jax.nn.sigmoid(dot(zn, gate_ref[u]))
        picks = picks_outgoing(core) if u == 0 else picks_incoming(core)

        for side in range(2):
            arrived(recvz.at[u, side], zr.at[u, side])

            def spread_plane(p, carry, side=side, u=u):
                tiles = [recvz[u, side, p, :, t * 128 : t * 128 + 128].astype(F32) for t in range(5)]
                for r, piece in enumerate(split_rows(tiles)):
                    spread[u, side, pl.ds(p * A + r, GROUP, stride=ROWS), :] = piece
                return carry

            lax.fori_loop(0, Z, spread_plane, 0)
            for x in range(XLO):
                for c in range(YX):
                    at = (c * XLO + x) * ROWS
                    sendp[u, side, x * YX + c] = spread[u, side, at : at + ROWS, :].astype(BF16)
            over_chips(sendp.at[u, side], recvp.at[u, side, 0], ps.at[u, side], pr.at[u, side])

        for side in range(2):
            arrived(recvp.at[u, side, 0], pr.at[u, side])
            if u == 0 or side == 0:
                remote(recvp.at[u, side, 0], recvp.at[u, side, 1], cs.at[u, side], cr.at[u, side], other_core)

        def blocks(side, cores):
            return jnp.concatenate(
                [recvp[u, side, k, x * YX : x * YX + YX].reshape(YX * ROWS, 128) for k in range(cores) for x in range(XLO)], axis=1
            )

        arrived(recvp.at[u, 0, 1], cr.at[u, 0])
        if u == 0:
            arrived(recvp.at[u, 1, 1], cr.at[u, 1])
            right = dot(picks, blocks(1, 2)).astype(BF16)
            tri = dot(blocks(0, 2), right, NT)
        else:
            left = dot(picks, blocks(0, 2), NT).astype(BF16)
            tri = dot(left, blocks(1, 1))
        for x in range(XLO):
            sendq[u, x * YX : x * YX + YX] = tri[:, x * 128 : x * 128 + 128].astype(BF16).reshape(YX, ROWS, 128)
        over_chips(sendq.at[u], recvq.at[u], qs.at[u], qr.at[u])

        arrived(recvq.at[u], qr.at[u])
        for x in range(XLO):
            for c in range(YX):
                at = (c * XLO + x) * ROWS
                gather[u, at : at + ROWS, :] = recvq[u, x * YX + c].astype(F32)

        def gather_plane(p, carry, u=u):
            pieces = [gather[u, pl.ds(p * A + r, GROUP, stride=ROWS), :] for r in range(A)]
            for t, tile in enumerate(join_rows(pieces)):
                sendx[u, p, :, t * 128 : t * 128 + 128] = tile.astype(BF16)
            return carry

        lax.fori_loop(0, Z, gather_plane, 0)
        over_planes(sendx.at[u], recvx.at[u], xs.at[u], xr.at[u])
        arrived(recvx.at[u], xr.at[u])
        tri = recvx[u].reshape(C, LANES)[:, 0:POS].astype(F32)
        tn = normed(tri, 0).astype(BF16)
        pair = pair + gate * dot(tn, out_ref[u], TN)
    o_ref[...] = pair.reshape(A, B, C)

    for u in range(2):
        for side in range(2):
            arrived(recvz.at[u, side, pl.ds(0, Z - 1)], zs.at[u, side])
            arrived(recvp.at[u, side, 0, pl.ds(0, CHIPS - 1)], ps.at[u, side])
            if u == 0 or side == 0:
                arrived(recvp.at[u, side, 1], cs.at[u, side])
        arrived(recvq.at[u, pl.ds(0, CHIPS - 1)], qs.at[u])
        arrived(recvx.at[u, pl.ds(0, Z - 1)], xs.at[u])


def solution(mesh):
    vmem = pl.BlockSpec(memory_space=pltpu.VMEM)

    def per_device(pair_rep, proj_weights, gate_weights, out_weights):
        return pl.pallas_call(
            kernel,
            out_shape=jax.ShapeDtypeStruct(pair_rep.shape, pair_rep.dtype),
            in_specs=[vmem] * 4,
            out_specs=vmem,
            scratch_shapes=[
                pltpu.VMEM((2, 2, Z, GROUP, LANES), BF16),
                pltpu.VMEM((2, 2, Z, GROUP, LANES), BF16),
                pltpu.VMEM((2, 2, GROUP * ROWS, 128), F32),
                pltpu.VMEM((2, 2, CHIPS, ROWS, 128), BF16),
                pltpu.VMEM((2, 2, CORES, CHIPS, ROWS, 128), BF16),
                pltpu.VMEM((2, CHIPS, ROWS, 128), BF16),
                pltpu.VMEM((2, CHIPS, ROWS, 128), BF16),
                pltpu.VMEM((2, GROUP * ROWS, 128), F32),
                pltpu.VMEM((2, Z, GROUP, LANES), BF16),
                pltpu.VMEM((2, Z, GROUP, LANES), BF16),
            ]
            + [pltpu.SemaphoreType.DMA((2, 2))] * 6
            + [pltpu.SemaphoreType.DMA((2,))] * 4,
            compiler_params=pltpu.CompilerParams(
                collective_id=0, has_side_effects=True, vmem_limit_bytes=48 * 1024 * 1024
            ),
        )(pair_rep, proj_weights, gate_weights, out_weights)

    return jax.shard_map(
        per_device,
        mesh=mesh,
        in_specs=(P("row", "col", None), P(), P(), P()),
        out_specs=P("row", "col", None),
        check_vma=False,
    )
```

time: 128 us -> 73.5 us (0.57)
  the two profiles are of different devices: /device:TPU:1 before, /device:TPU:32 now
where the time goes in v2:
time: 73.5 us; the launch traced here: 73.2 us
  Pallas kernels  68.9 us (94%)
  local copies, waits for them, and re-layouts  4.3 us (6%)
    pallas_call x1, Pallas kernels, per_device(): pl.pallas_call(kernel, out_shape=jax.ShapeDtypeStruct(pair_rep.shape, pai...  68.9 us
    unnamed x9, local copies, waits for them, and re-layouts  4.3 us

profile of v2, /device:TPU:32, one launch (start us, length us, event | category | flops | bytes accessed | tf_op | source)
XLA Modules:
  0.0 73.2 jit_solution(13364462404177989461)
XLA Ops:
  0.0 0.0 copy-start
  0.0 1.0 %copy-done = f32[6,96,128]{2,1,0:T(8,128)S(1)} copy-done((f32[6,96,128]{2,1,0:T(8,128)S(1)}, f32[6,96,128]{2,1,0:T(8,128)}, u32[]{:S(2)}) %copy-start) | copy-done | bytes 294936
  1.0 0.0 copy-start.1
  1.0 0.9 %copy-done.1 = bf16[2,4,128,128]{3,2,1,0:T(8,128)(2,1)S(1)} copy-done((bf16[2,4,128,128]{3,2,1,0:T(8,128)(2,1)S(1)}, bf16[2,4,128,128]{3,2,1,0:T(8,128)(2,1)}, u32[]{:S(2)}) %copy-start.1) | copy-done | bytes 262168
  1.9 0.0 copy-start.2
  1.9 0.8 %copy-done.2 = bf16[2,128,128]{2,1,0:T(8,128)(2,1)S(1)} copy-done((bf16[2,128,128]{2,1,0:T(8,128)(2,1)S(1)}, bf16[2,128,128]{2,1,0:T(8,128)(2,1)}, u32[]{:S(2)}) %copy-start.2) | copy-done | bytes 65560
  2.8 0.0 copy-start.3
  2.8 0.8 %copy-done.3 = bf16[2,128,128]{2,1,0:T(8,128)(2,1)S(1)} copy-done((bf16[2,128,128]{2,1,0:T(8,128)(2,1)S(1)}, bf16[2,128,128]{2,1,0:T(8,128)(2,1)}, u32[]{:S(2)}) %copy-start.3) | copy-done | bytes 65560
  3.6 68.9 %shard_map.46 = f32[6,96,128]{2,1,0:T(8,128)S(1)} custom-call(f32[6,96,128]{2,1,0:T(8,128)S(1)} %copy-done, bf16[2,4,128,128]{3,2,1,0:T(8,128)(2,1)S(1)} %copy-done.1, bf16[2,128,128]{2,1,0:T(8,128)(2,1)S(1)} %copy-done.2, bf16[2,128,128]{2,1,0:T(8,128)(2,1)S(1)} %copy-done.3), custom_call_target="tpu_custom_call" | custom-call | tf_op jit(solution)/shard_map/pallas_call | solution.py:210
  72.5 0.7 copy.6
Async XLA Ops:
  0.0 1.0 %copy-start = (f32[6,96,128]{2,1,0:T(8,128)S(1)}, f32[6,96,128]{2,1,0:T(8,128)}, u32[]{:S(2)}) copy-start(f32[6,96,128]{2,1,0:T(8,128)} %z_ref.1) | copy-start | bytes 884740
  1.0 0.9 %copy-start.1 = (bf16[2,4,128,128]{3,2,1,0:T(8,128)(2,1)S(1)}, bf16[2,4,128,128]{3,2,1,0:T(8,128)(2,1)}, u32[]{:S(2)}) copy-start(bf16[2,4,128,128]{3,2,1,0:T(8,128)(2,1)} %proj_ref.1) | copy-start | bytes 786436
  1.9 0.8 %copy-start.2 = (bf16[2,128,128]{2,1,0:T(8,128)(2,1)S(1)}, bf16[2,128,128]{2,1,0:T(8,128)(2,1)}, u32[]{:S(2)}) copy-start(bf16[2,128,128]{2,1,0:T(8,128)(2,1)} %gate_ref.1) | copy-start | bytes 196612
  2.8 0.8 %copy-start.3 = (bf16[2,128,128]{2,1,0:T(8,128)(2,1)S(1)}, bf16[2,128,128]{2,1,0:T(8,128)(2,1)}, u32[]{:S(2)}) copy-start(bf16[2,128,128]{2,1,0:T(8,128)(2,1)} %out_ref.1) | copy-start | bytes 196612

commit v3 on v2

v3 whole, which is shorter than its diff:
```python
import jax
import jax.numpy as jnp
from jax import lax
from jax.experimental import pallas as pl
from jax.experimental.pallas import tpu as pltpu
from jax.sharding import PartitionSpec as P

MESH = pl.DeviceIdType.MESH
F32, BF16 = jnp.float32, jnp.bfloat16
Z, CHIPS, YX, XLO, CORES = 8, 16, 8, 2, 2
A, B, C = 6, 96, 128
HALF = 8
POS, LANES = A * B, 640
ROWS = Z * A
FAR_PLANES = (4, 3, 5, 2, 6, 1, 7)
FAR_CHIPS = (10, 11, 9, 14, 6, 8, 2, 15, 13, 7, 5, 12, 4, 3, 1)
FAR_YX = (5, 7, 3, 4, 1, 6, 2, 0)
NT = (((1,), (1,)), ((), ()))
TN = (((0,), (0,)), ((), ()))


def normed(values, axis):
    centred = values - jnp.mean(values, axis=axis, keepdims=True)
    variance = jnp.mean(centred * centred, axis=axis, keepdims=True)
    return centred * lax.rsqrt(variance + 1e-05)


def dot(a, b, dims=(((1,), (0,)), ((), ()))):
    return lax.dot_general(a, b, dims, preferred_element_type=F32)


def lane_of(rows):
    return lax.broadcasted_iota(jnp.int32, (rows, 128), 1)


def split_rows(tiles):
    lane = lane_of(tiles[0].shape[0])
    t0, t1, t2, t3, t4 = tiles
    pieces = [
        t0,
        pltpu.roll(jnp.where(lane < 64, t1, t0), 32, 1),
        pltpu.roll(jnp.where(lane < 32, t2, t1), 64, 1),
        pltpu.roll(t2, 96, 1),
        t3,
        pltpu.roll(jnp.where(lane < 64, t4, t3), 32, 1),
    ]
    return [jnp.where(lane < B, piece, 0.0) for piece in pieces]


def picks_outgoing(core):
    row = lax.broadcasted_iota(jnp.int32, (XLO * 128, YX * ROWS), 0)
    col = lax.broadcasted_iota(jnp.int32, (XLO * 128, YX * ROWS), 1)
    x_lo, jr = row // 128, row % 128
    z = 4 * x_lo + 2 * core + jr // 48
    source = (jr % 48) // A * ROWS + z * A + jr % A
    return jnp.where((col == source) & (jr < B), 1.0, 0.0).astype(BF16)


def picks_incoming(core):
    row = lax.broadcasted_iota(jnp.int32, (YX * ROWS, 4 * 128), 0)
    col = lax.broadcasted_iota(jnp.int32, (YX * ROWS, 4 * 128), 1)
    yx, z, r = row // ROWS, row % ROWS // A, row % A
    other = jnp.bitwise_xor((z // 2) % 2, core)
    source = (other * 2 + z // 4) * 128 + (z % 2) * 48 + yx * A + r
    return jnp.where(col == source, 1.0, 0.0).astype(BF16)


def kernel(
    pair_hbm, proj_hbm, gate_hbm, out_hbm, o_ref,
    z_ref, proj_ref, gate_ref, out_ref, wide,
    sendz, recvz, spread, sendp, recvp, sendq, recvq, gather, sendx, recvx,
    load, zs, zr, ps, pr, cs, cr, qs, qr, xs, xr,
):
    loads = [
        pltpu.make_async_copy(src, dst, load.at[i])
        for i, (src, dst) in enumerate(
            ((pair_hbm, z_ref), (proj_hbm, proj_ref), (gate_hbm, gate_ref), (out_hbm, out_ref))
        )
    ]
    loads[0].start()
    loads[1].start()
    row, col = lax.axis_index("row"), lax.axis_index("col")
    plane, yx, x_lo, core = row >> 3, row & 7, col >> 1, col & 1
    chip = yx * XLO + x_lo
    chunk_of_chip = x_lo ^ ((yx >> 1) & 1)
    planes = [(plane + s) & (Z - 1) for s in FAR_PLANES]
    chips = [chip ^ s for s in FAR_CHIPS]

    def on_plane(other_plane):
        return {"row": other_plane * YX + yx, "col": col}

    def on_chip(other_chip):
        return {"row": plane * YX + (other_chip >> 1), "col": (other_chip & 1) * CORES + core}

    other_core = {"row": row, "col": col ^ 1}

    barrier = pltpu.get_barrier_semaphore()
    peers = [on_plane(peer) for peer in planes] + [on_chip(peer) for peer in chips] + [other_core]
    for peer in peers:
        pl.semaphore_signal(barrier, inc=1, device_id=peer, device_id_type=MESH)
    loads[2].start()
    loads[3].start()

    sent = []

    def remote(src, dst, send, recv, peer):
        pltpu.make_async_remote_copy(
            src_ref=src, dst_ref=dst, send_sem=send, recv_sem=recv, device_id=peer, device_id_type=MESH
        ).start()

    def arrived(ref, sem):
        pltpu.make_async_copy(ref, ref, sem).wait()

    def slot_of(some_chip):
        return (some_chip & 1) * YX + (some_chip >> 1)

    def over_planes(src, dst, send, recv):
        for peer in planes:
            remote(src.at[peer], dst.at[plane], send, recv, on_plane(peer))
        pltpu.make_async_copy(src.at[plane], dst.at[plane], recv).start()
        sent.append((src.at[pl.ds(0, Z - 1)], send))

    def to_owners(chunk, src, dst, send, recv):
        here = dst.at[slot_of(chip)]
        for s in FAR_YX[:-1]:
            peer = yx ^ s
            remote(src.at[peer], here, send, recv, on_chip(peer * XLO + (chunk ^ ((peer >> 1) & 1))))
        own = chunk_of_chip == chunk

        @pl.when(own)
        def _():
            pltpu.make_async_copy(src.at[yx], here, recv).start()

        @pl.when(jnp.logical_not(own))
        def _():
            remote(src.at[yx], here, send, recv, on_chip(chip ^ 1))

    def wide_weights(u):
        for i in range(4):
            turned = proj_ref[u, i].astype(F32).T.reshape(Z, 2, HALF, C)
            for k in range(2):
                wide[u, k, i] = turned[:, k].reshape(Z * HALF, C).astype(BF16)

    def update(u, pair):
        zn = normed(pair, -1).astype(BF16)
        for k in range(2):
            both = dot(wide[u, k].reshape(4 * Z * HALF, C), zn, NT).reshape(4, Z, HALF, POS)
            left = jax.nn.sigmoid(both[0]) * both[1]
            right = jax.nn.sigmoid(both[2]) * both[3]
            sendz[u, k, :, :, 0:POS] = jnp.concatenate([left, right], axis=1).astype(BF16)
            if u == 0 and k == 0:
                pl.semaphore_wait(barrier, len(peers))
            over_planes(sendz.at[u, k], recvz.at[u, k], zs.at[u, k], zr.at[u, k])
        if u == 0:
            wide_weights(1)
            loads[2].wait()
            loads[3].wait()
        gate = jax.nn.sigmoid(dot(zn, gate_ref[u]))
        picks = picks_outgoing(core) if u == 0 else picks_incoming(core)

        for k in range(2):
            arrived(recvz.at[u, k], zr.at[u, k])

            def spread_plane(p, carry):
                tiles = [recvz[u, k, p, :, t * 128 : t * 128 + 128].astype(F32) for t in range(5)]
                for r, piece in enumerate(split_rows(tiles)):
                    spread[u, k, pl.ds(p * A + r, 2 * HALF, stride=ROWS), :] = piece
                return carry

            lax.fori_loop(0, Z, spread_plane, 0, unroll=2)
            for side in range(2):
                for m in range(HALF):
                    at = (side * HALF + m) * ROWS
                    sendp[u, k, m, side] = spread[u, k, at : at + ROWS, :].astype(BF16)
            to_owners(k, sendp.at[u, k], recvp.at[u, 0], ps.at[u], pr.at[u])
        sent.append((recvp.at[u, 0, pl.ds(0, CHIPS - 1)], ps.at[u]))

        arrived(recvp.at[u, 0], pr.at[u])
        for side in range(2 if u == 0 else 1):
            src = recvp.at[u, 0, :, side]
            remote(src, recvp.at[u, 1, :, side], cs.at[u, side], cr.at[u, side], other_core)
            sent.append((src, cs.at[u, side]))
        for side in range(2 if u == 0 else 1):
            arrived(recvp.at[u, 1, :, side], cr.at[u, side])

        def blocks(side, cores):
            return jnp.concatenate(
                [
                    recvp[u, k, x * YX : x * YX + YX, side].reshape(YX * ROWS, 128)
                    for k in range(cores)
                    for x in range(XLO)
                ],
                axis=1,
            )

        if u == 0:
            right = dot(picks, blocks(1, 2)).astype(BF16)
            tri = dot(blocks(0, 2), right, NT)
        else:
            left = dot(picks, blocks(0, 2), NT).astype(BF16)
            tri = dot(left, blocks(1, 1))
        for x in range(XLO):
            sendq[u, x * YX : x * YX + YX] = tri[:, x * 128 : x * 128 + 128].astype(BF16).reshape(YX, ROWS, 128)
        here = recvq.at[u, chunk_of_chip, yx]
        for peer in chips:
            remote(sendq.at[u, slot_of(peer)], here, qs.at[u], qr.at[u, chunk_of_chip], on_chip(peer))
        pltpu.make_async_copy(sendq.at[u, slot_of(chip)], here, qr.at[u, chunk_of_chip]).start()
        sent.append((sendq.at[u, pl.ds(0, CHIPS - 1)], qs.at[u]))

        for k in range(2):
            arrived(recvq.at[u, k], qr.at[u, k])
            gather[u, k] = recvq[u, k].reshape(HALF * ROWS, 128).astype(F32)

            def gather_plane(p, carry):
                for r in range(0, A, 2):
                    pair_of_rows = [gather[u, k, pl.ds(p * A + r + i, HALF, stride=ROWS), :] for i in range(2)]
                    sendx[u, k, p, r * HALF : r * HALF + 2 * HALF] = jnp.concatenate(pair_of_rows, axis=0).astype(BF16)
                return carry

            lax.fori_loop(0, Z, gather_plane, 0, unroll=2)
            over_planes(sendx.at[u, k], recvx.at[u, k], xs.at[u, k], xr.at[u, k])
        for k in range(2):
            arrived(recvx.at[u, k], xr.at[u, k])
        tri = [recvx[u, k, p].astype(F32) for p in range(Z) for k in range(2)]
        for r in range(A):
            tri_row = jnp.concatenate([part[r * HALF : r * HALF + HALF] for part in tri], axis=0)
            projected = dot(normed(tri_row, 0).astype(BF16), out_ref[u], TN)[:B]
            rows = slice(r * B, r * B + B)
            o_ref[r] = pair[rows] + gate[rows] * projected

    loads[1].wait()
    wide_weights(0)
    loads[0].wait()
    update(0, z_ref[...].reshape(POS, C))
    update(1, o_ref[...].reshape(POS, C))
    for ref, sem in sent:
        arrived(ref, sem)


def solution(mesh):
    vmem = pl.BlockSpec(memory_space=pltpu.VMEM)

    def per_device(pair_rep, proj_weights, gate_weights, out_weights):
        return pl.pallas_call(
            kernel,
            out_shape=jax.ShapeDtypeStruct(pair_rep.shape, pair_rep.dtype),
            in_specs=[pl.BlockSpec(memory_space=pltpu.HBM)] * 4,
            out_specs=vmem,
            scratch_shapes=[
                pltpu.VMEM(pair_rep.shape, F32),
                pltpu.VMEM(proj_weights.shape, BF16),
                pltpu.VMEM(gate_weights.shape, BF16),
                pltpu.VMEM(out_weights.shape, BF16),
                pltpu.VMEM((2, 2, 4, Z * HALF, C), BF16),
                pltpu.VMEM((2, 2, Z, 2 * HALF, LANES), BF16),
                pltpu.VMEM((2, 2, Z, 2 * HALF, LANES), BF16),
                pltpu.VMEM((2, 2, 2 * HALF * ROWS, 128), F32),
                pltpu.VMEM((2, 2, HALF, 2, ROWS, 128), BF16),
                pltpu.VMEM((2, CORES, CHIPS, 2, ROWS, 128), BF16),
                pltpu.VMEM((2, CHIPS, ROWS, 128), BF16),
                pltpu.VMEM((2, 2, HALF, ROWS, 128), BF16),
                pltpu.VMEM((2, 2, HALF * ROWS, 128), F32),
                pltpu.VMEM((2, 2, Z, A * HALF, 128), BF16),
                pltpu.VMEM((2, 2, Z, A * HALF, 128), BF16),
                pltpu.SemaphoreType.DMA((4,)),
                pltpu.SemaphoreType.DMA((2, 2)),
                pltpu.SemaphoreType.DMA((2, 2)),
                pltpu.SemaphoreType.DMA((2,)),
                pltpu.SemaphoreType.DMA((2,)),
                pltpu.SemaphoreType.DMA((2, 2)),
                pltpu.SemaphoreType.DMA((2, 2)),
                pltpu.SemaphoreType.DMA((2,)),
                pltpu.SemaphoreType.DMA((2, 2)),
                pltpu.SemaphoreType.DMA((2, 2)),
                pltpu.SemaphoreType.DMA((2, 2)),
            ],
            compiler_params=pltpu.CompilerParams(
                collective_id=0, has_side_effects=True, vmem_limit_bytes=(65536 - 256) * 1024
            ),
        )(pair_rep, proj_weights, gate_weights, out_weights)

    return jax.shard_map(
        per_device,
        mesh=mesh,
        in_specs=(P("row", "col", None), P(), P(), P()),
        out_specs=P("row", "col", None),
        check_vma=False,
    )
```

time: 73.5 us -> 67.7 us (0.921)
  the two profiles are of different devices: /device:TPU:32 before, /device:TPU:1 now
where the time goes in v3:
time: 67.7 us; the launch traced here: 67.6 us
  Pallas kernels  65.9 us (97%)
  local copies, waits for them, and re-layouts  1.69 us (2%)
    pallas_call x1, Pallas kernels, per_device(): pl.pallas_call(kernel, out_shape=jax.ShapeDtypeStruct(pair_rep.shape, pai...  65.9 us
    unnamed x1, local copies, waits for them, and re-layouts  1.69 us

profile of v3, /device:TPU:1, one launch (start us, length us, event | category | flops | bytes accessed | tf_op | source)
XLA Modules:
  0.0 67.6 jit_solution(2212954235027577943)
XLA Ops:
  0.0 65.9 %shard_map.46 = f32[6,96,128]{2,1,0:T(8,128)} custom-call(f32[6,96,128]{2,1,0:T(8,128)} %pair_hbm.1, bf16[2,4,128,128]{3,2,1,0:T(8,128)(2,1)} %proj_hbm.1, bf16[2,128,128]{2,1,0:T(8,128)(2,1)} %gate_hbm.1, bf16[2,128,128]{2,1,0:T(8,128)(2,1)} %out_hbm.1), custom_call_target="tpu_custom_call" | custom-call | tf_op jit(solution)/shard_map/pallas_call | solution.py:244
  65.9 1.7 %copy.6 = f32[6,96,128]{2,1,0:T(8,128)} copy(f32[6,96,128]{2,1,0:T(8,128)} %shard_map.46) | data formatting | bytes 589824

commit v4 on v3

--- a/solution.py
+++ b/solution.py
@@ -10,10 +10,11 @@
 Z, CHIPS, YX, XLO, CORES = 8, 16, 8, 2, 2
 A, B, C = 6, 96, 128
 HALF = 8
-POS, LANES = A * B, 640
+POS = A * B
 ROWS = Z * A
 FAR_PLANES = (4, 3, 5, 2, 6, 1, 7)
 FAR_CHIPS = (10, 11, 9, 14, 6, 8, 2, 15, 13, 7, 5, 12, 4, 3, 1)
+SIGNAL_ORDER = (0, 7, 1, 2, 8, 9, 10, 11, 3, 4, 12, 13, 14, 15, 16, 17, 5, 6, 18, 19, 20, 21, 22)
 FAR_YX = (5, 7, 3, 4, 1, 6, 2, 0)
 NT = (((1,), (1,)), ((), ()))
 TN = (((0,), (0,)), ((), ()))
@@ -33,33 +34,44 @@
     return lax.broadcasted_iota(jnp.int32, (rows, 128), 1)
 
 
-def split_rows(tiles):
+def rows_of_a(tiles):
     lane = lane_of(tiles[0].shape[0])
-    t0, t1, t2, t3, t4 = tiles
+    t0, t1, t2 = tiles
     pieces = [
         t0,
         pltpu.roll(jnp.where(lane < 64, t1, t0), 32, 1),
         pltpu.roll(jnp.where(lane < 32, t2, t1), 64, 1),
         pltpu.roll(t2, 96, 1),
-        t3,
-        pltpu.roll(jnp.where(lane < 64, t4, t3), 32, 1),
     ]
     return [jnp.where(lane < B, piece, 0.0) for piece in pieces]
+
+
+def rows_of_b(tile, tail, tail_at):
+    lane = lane_of(tile.shape[0])
+    fifth = jnp.where(lane < 32, pltpu.roll(tile, 32, 1), pltpu.roll(tail, (32 - tail_at) % 128, 1))
+    return [jnp.where(lane < B, piece, 0.0) for piece in (tile, fifth)]
+
+
+def place(z, r, part):
+    return z * 4 + r if part == 0 else 32 + z * 2 + r - 4
 
 
 def picks_outgoing(core):
     row = lax.broadcasted_iota(jnp.int32, (XLO * 128, YX * ROWS), 0)
     col = lax.broadcasted_iota(jnp.int32, (XLO * 128, YX * ROWS), 1)
     x_lo, jr = row // 128, row % 128
-    z = 4 * x_lo + 2 * core + jr // 48
-    source = (jr % 48) // A * ROWS + z * A + jr % A
+    z, yx, r = 4 * x_lo + 2 * core + jr // 48, jr % 48 // A, jr % A
+    source = jnp.where(r < 4, yx * 32 + z * 4 + r, 256 + yx * 16 + z * 2 + r - 4)
     return jnp.where((col == source) & (jr < B), 1.0, 0.0).astype(BF16)
 
 
 def picks_incoming(core):
     row = lax.broadcasted_iota(jnp.int32, (YX * ROWS, 4 * 128), 0)
     col = lax.broadcasted_iota(jnp.int32, (YX * ROWS, 4 * 128), 1)
-    yx, z, r = row // ROWS, row % ROWS // A, row % A
+    in_a, late = row < 256, row - 256
+    yx = jnp.where(in_a, row // 32, late // 16)
+    z = jnp.where(in_a, row % 32 // 4, late % 16 // 2)
+    r = jnp.where(in_a, row % 4, 4 + late % 2)
     other = jnp.bitwise_xor((z // 2) % 2, core)
     source = (other * 2 + z // 4) * 128 + (z % 2) * 48 + yx * A + r
     return jnp.where(col == source, 1.0, 0.0).astype(BF16)
@@ -68,7 +80,7 @@
 def kernel(
     pair_hbm, proj_hbm, gate_hbm, out_hbm, o_ref,
     z_ref, proj_ref, gate_ref, out_ref, wide,
-    sendz, recvz, spread, sendp, recvp, sendq, recvq, gather, sendx, recvx,
+    senda, recva, send2, recv2, send1, recv1, spread, sendpa, sendpb, recvpa, recvpb, sendq, recvq, gather, sendx, recvx,
     load, zs, zr, ps, pr, cs, cr, qs, qr, xs, xr,
 ):
     loads = [
@@ -96,6 +108,7 @@
 
     barrier = pltpu.get_barrier_semaphore()
     peers = [on_plane(peer) for peer in planes] + [on_chip(peer) for peer in chips] + [other_core]
+    peers = [peers[i] for i in SIGNAL_ORDER]
     for peer in peers:
         pl.semaphore_signal(barrier, inc=1, device_id=peer, device_id_type=MESH)
     loads[2].start()
@@ -143,14 +156,28 @@
 
     def update(u, pair):
         zn = normed(pair, -1).astype(BF16)
-        for k in range(2):
-            both = dot(wide[u, k].reshape(4 * Z * HALF, C), zn, NT).reshape(4, Z, HALF, POS)
+
+        def edges(k, some):
+            both = dot(wide[u, k].reshape(4 * Z * HALF, C), some, NT).reshape(4, Z, HALF, some.shape[0])
             left = jax.nn.sigmoid(both[0]) * both[1]
             right = jax.nn.sigmoid(both[2]) * both[3]
-            sendz[u, k, :, :, 0:POS] = jnp.concatenate([left, right], axis=1).astype(BF16)
-            if u == 0 and k == 0:
-                pl.semaphore_wait(barrier, len(peers))
-            over_planes(sendz.at[u, k], recvz.at[u, k], zs.at[u, k], zr.at[u, k])
+            return jnp.concatenate([left, right], axis=1).astype(BF16)
+
+        z_parts = [(senda.at[u, 0], recva.at[u, 0]), (send2.at[u], recv2.at[u])]
+        z_parts += [(senda.at[u, 1], recva.at[u, 1]), (send1.at[u], recv1.at[u])]
+        first = edges(0, zn)
+        senda[u, 0] = first[:, :, 0:384]
+        if u == 0:
+            pl.semaphore_wait(barrier, len(peers))
+        over_planes(*z_parts[0], zs.at[u, 0], zr.at[u, 0])
+        send2[u, :, :, 0:192] = first[:, :, 384:POS]
+        send2[u, :, :, 192:256] = edges(1, zn[512:POS])
+        over_planes(*z_parts[1], zs.at[u, 1], zr.at[u, 1])
+        second = edges(1, zn[0:512])
+        senda[u, 1] = second[:, :, 0:384]
+        send1[u] = second[:, :, 384:512]
+        over_planes(*z_parts[2], zs.at[u, 2], zr.at[u, 2])
+        over_planes(*z_parts[3], zs.at[u, 3], zr.at[u, 3])
         if u == 0:
             wide_weights(1)
             loads[2].wait()
@@ -159,34 +186,49 @@
         picks = picks_outgoing(core) if u == 0 else picks_incoming(core)
 
         for k in range(2):
-            arrived(recvz.at[u, k], zr.at[u, k])
-
-            def spread_plane(p, carry):
-                tiles = [recvz[u, k, p, :, t * 128 : t * 128 + 128].astype(F32) for t in range(5)]
-                for r, piece in enumerate(split_rows(tiles)):
-                    spread[u, k, pl.ds(p * A + r, 2 * HALF, stride=ROWS), :] = piece
-                return carry
-
-            lax.fori_loop(0, Z, spread_plane, 0, unroll=2)
-            for side in range(2):
-                for m in range(HALF):
-                    at = (side * HALF + m) * ROWS
-                    sendp[u, k, m, side] = spread[u, k, at : at + ROWS, :].astype(BF16)
-            to_owners(k, sendp.at[u, k], recvp.at[u, 0], ps.at[u], pr.at[u])
-        sent.append((recvp.at[u, 0, pl.ds(0, CHIPS - 1)], ps.at[u]))
-
-        arrived(recvp.at[u, 0], pr.at[u])
-        for side in range(2 if u == 0 else 1):
-            src = recvp.at[u, 0, :, side]
-            remote(src, recvp.at[u, 1, :, side], cs.at[u, side], cr.at[u, side], other_core)
-            sent.append((src, cs.at[u, side]))
-        for side in range(2 if u == 0 else 1):
-            arrived(recvp.at[u, 1, :, side], cr.at[u, side])
+            for part in range(2):
+                arrived(z_parts[2 * k + part][1], zr.at[u, 2 * k + part])
+
+                def spread_plane(p, carry):
+                    if part == 0:
+                        tiles = [recva[u, k, p, :, t * 128 : t * 128 + 128].astype(F32) for t in range(3)]
+                        pieces = rows_of_a(tiles)
+                    else:
+                        tile = recv2[u, p, :, 0:128] if k == 0 else recv1[u, p]
+                        pieces = rows_of_b(tile.astype(F32), recv2[u, p, :, 128:256].astype(F32), 64 * k)
+                    for i, piece in enumerate(pieces):
+                        spread[u, k, pl.ds(place(p, 4 * part + i, part), 2 * HALF, stride=ROWS), :] = piece
+                    return carry
+
+                lax.fori_loop(0, Z, spread_plane, 0, unroll=2)
+                sendp, lo, hi = (sendpa, 0, 32) if part == 0 else (sendpb, 32, ROWS)
+                for side in range(2):
+                    for m in range(HALF):
+                        at = (side * HALF + m) * ROWS
+                        sendp[u, k, m, side] = spread[u, k, at + lo : at + hi, :].astype(BF16)
+                recvp = (recvpa, recvpb)[part]
+                to_owners(k, sendp.at[u, k], recvp.at[u, 0], ps.at[u, part], pr.at[u, part])
+
+        sides = pl.ds(0, 2 if u == 0 else 1)
+        for part, recvp in enumerate((recvpa, recvpb)):
+            sent.append((recvp.at[u, 0, pl.ds(0, CHIPS - 1)], ps.at[u, part]))
+            arrived(recvp.at[u, 0], pr.at[u, part])
+            src = recvp.at[u, 0, :, sides]
+            remote(src, recvp.at[u, 1, :, sides], cs.at[u, part], cr.at[u, part], other_core)
+            sent.append((src, cs.at[u, part]))
+        for part, recvp in enumerate((recvpa, recvpb)):
+            arrived(recvp.at[u, 1, :, sides], cr.at[u, part])
 
         def blocks(side, cores):
             return jnp.concatenate(
                 [
-                    recvp[u, k, x * YX : x * YX + YX, side].reshape(YX * ROWS, 128)
+                    jnp.concatenate(
+                        [
+                            recvpa[u, k, x * YX : x * YX + YX, side].reshape(256, 128),
+                            recvpb[u, k, x * YX : x * YX + YX, side].reshape(128, 128),
+                        ],
+                        axis=0,
+                    )
                     for k in range(cores)
                     for x in range(XLO)
                 ],
@@ -200,7 +242,9 @@
             left = dot(picks, blocks(0, 2), NT).astype(BF16)
             tri = dot(left, blocks(1, 1))
         for x in range(XLO):
-            sendq[u, x * YX : x * YX + YX] = tri[:, x * 128 : x * 128 + 128].astype(BF16).reshape(YX, ROWS, 128)
+            block = tri[:, x * 128 : x * 128 + 128].astype(BF16)
+            sendq[u, x * YX : x * YX + YX, 0:32] = block[0:256].reshape(YX, 32, 128)
+            sendq[u, x * YX : x * YX + YX, 32:ROWS] = block[256:384].reshape(YX, 16, 128)
         here = recvq.at[u, chunk_of_chip, yx]
         for peer in chips:
             remote(sendq.at[u, slot_of(peer)], here, qs.at[u], qr.at[u, chunk_of_chip], on_chip(peer))
@@ -213,7 +257,9 @@
 
             def gather_plane(p, carry):
                 for r in range(0, A, 2):
-                    pair_of_rows = [gather[u, k, pl.ds(p * A + r + i, HALF, stride=ROWS), :] for i in range(2)]
+                    pair_of_rows = [
+                        gather[u, k, pl.ds(place(p, r + i, r // 4), HALF, stride=ROWS), :] for i in range(2)
+                    ]
                     sendx[u, k, p, r * HALF : r * HALF + 2 * HALF] = jnp.concatenate(pair_of_rows, axis=0).astype(BF16)
                 return carry
 
@@ -240,7 +286,8 @@
 def solution(mesh):
     vmem = pl.BlockSpec(memory_space=pltpu.VMEM)
 
-    def per_device(pair_rep, proj_weights, gate_weights, out_weights):
+    def per_device(*operands):
+        pair_rep, proj_weights, gate_weights, out_weights = operands
         return pl.pallas_call(
             kernel,
             out_shape=jax.ShapeDtypeStruct(pair_rep.shape, pair_rep.dtype),
@@ -252,21 +299,27 @@
                 pltpu.VMEM(gate_weights.shape, BF16),
                 pltpu.VMEM(out_weights.shape, BF16),
                 pltpu.VMEM((2, 2, 4, Z * HALF, C), BF16),
-                pltpu.VMEM((2, 2, Z, 2 * HALF, LANES), BF16),
-                pltpu.VMEM((2, 2, Z, 2 * HALF, LANES), BF16),
+                pltpu.VMEM((2, 2, Z, 2 * HALF, 384), BF16),
+                pltpu.VMEM((2, 2, Z, 2 * HALF, 384), BF16),
+                pltpu.VMEM((2, Z, 2 * HALF, 256), BF16),
+                pltpu.VMEM((2, Z, 2 * HALF, 256), BF16),
+                pltpu.VMEM((2, Z, 2 * HALF, 128), BF16),
+                pltpu.VMEM((2, Z, 2 * HALF, 128), BF16),
                 pltpu.VMEM((2, 2, 2 * HALF * ROWS, 128), F32),
-                pltpu.VMEM((2, 2, HALF, 2, ROWS, 128), BF16),
-                pltpu.VMEM((2, CORES, CHIPS, 2, ROWS, 128), BF16),
+                pltpu.VMEM((2, 2, HALF, 2, 32, 128), BF16),
+                pltpu.VMEM((2, 2, HALF, 2, 16, 128), BF16),
+                pltpu.VMEM((2, CORES, CHIPS, 2, 32, 128), BF16),
+                pltpu.VMEM((2, CORES, CHIPS, 2, 16, 128), BF16),
                 pltpu.VMEM((2, CHIPS, ROWS, 128), BF16),
                 pltpu.VMEM((2, 2, HALF, ROWS, 128), BF16),
                 pltpu.VMEM((2, 2, HALF * ROWS, 128), F32),
                 pltpu.VMEM((2, 2, Z, A * HALF, 128), BF16),
                 pltpu.VMEM((2, 2, Z, A * HALF, 128), BF16),
                 pltpu.SemaphoreType.DMA((4,)),
-                pltpu.SemaphoreType.DMA((2, 2)),
-                pltpu.SemaphoreType.DMA((2, 2)),
-                pltpu.SemaphoreType.DMA((2,)),
-                pltpu.SemaphoreType.DMA((2,)),
+                pltpu.SemaphoreType.DMA((2, 4)),
+                pltpu.SemaphoreType.DMA((2, 4)),
+                pltpu.SemaphoreType.DMA((2, 2)),
+                pltpu.SemaphoreType.DMA((2, 2)),
                 pltpu.SemaphoreType.DMA((2, 2)),
                 pltpu.SemaphoreType.DMA((2, 2)),
                 pltpu.SemaphoreType.DMA((2,)),
@@ -275,9 +328,9 @@
                 pltpu.SemaphoreType.DMA((2, 2)),
             ],
             compiler_params=pltpu.CompilerParams(
-                collective_id=0, has_side_effects=True, vmem_limit_bytes=(65536 - 256) * 1024
+                collective_id=0, has_side_effects=True, vmem_limit_bytes=48 * 1024 * 1024
             ),
-        )(pair_rep, proj_weights, gate_weights, out_weights)
+        )(*(pltpu.with_memory_space_constraint(x, pltpu.HBM) for x in operands))
 
     return jax.shard_map(
         per_device,

time: 67.7 us -> 64.4 us (0.951)
  Pallas kernels: 65.9 us -> 63.6 us
  local copies, waits for them, and re-layouts: 1.69 us -> 0.72 us
    pallas_call x1, Pallas kernels: 65.9 us -> 63.6 us  [per_device(): pl.pallas_call(kernel, out_shape=jax.ShapeDtypeStruct(pair_rep.shape, pai...]
    unnamed x1, local copies, waits for them, and re-layouts: 1.69 us -> 0.72 us
where the time goes in v4:
time: 64.4 us; the launch traced here: 64.3 us
  Pallas kernels  63.6 us (99%)
  local copies, waits for them, and re-layouts  0.72 us (1%)
    pallas_call x1, Pallas kernels, per_device(): pl.pallas_call(kernel, out_shape=jax.ShapeDtypeStruct(pair_rep.shape, pai...  63.6 us

profile of v4, /device:TPU:1, one launch (start us, length us, event | category | flops | bytes accessed | tf_op | source)
XLA Modules:
  0.0 64.3 jit_solution(1630136319465467259)
XLA Ops:
  0.0 63.6 %shard_map.46 = f32[6,96,128]{2,1,0:T(8,128)S(1)} custom-call(f32[6,96,128]{2,1,0:T(8,128)} %pair_hbm.1, bf16[2,4,128,128]{3,2,1,0:T(8,128)(2,1)} %proj_hbm.1, bf16[2,128,128]{2,1,0:T(8,128)(2,1)} %gate_hbm.1, bf16[2,128,128]{2,1,0:T(8,128)(2,1)} %out_hbm.1), custom_call_target="tpu_custom_call" | custom-call | tf_op jit(solution)/shard_map/pallas_call | solution.py:291
  63.6 0.7 %copy.6 = f32[6,96,128]{2,1,0:T(8,128)} copy(f32[6,96,128]{2,1,0:T(8,128)S(1)} %shard_map.46) | data formatting | bytes 589824

commit v5 on v4

v5 whole, which is shorter than its diff:
```python
import jax
import jax.numpy as jnp
from jax import lax
from jax.experimental import pallas as pl
from jax.experimental.pallas import tpu as pltpu
from jax.sharding import PartitionSpec as P

MESH = pl.DeviceIdType.MESH
F32, BF16 = jnp.float32, jnp.bfloat16
Z, CHIPS, YX, XLO, CORES = 8, 16, 8, 2, 2
A, B, C = 6, 96, 128
HALF = 8
POS = A * B
ROWS = Z * A
FAR_PLANES = (4, 3, 5, 2, 6, 1, 7)
FAR_CHIPS = (10, 11, 9, 14, 6, 8, 2, 15, 13, 7, 5, 12, 4, 3, 1)
PLANE_HOPS = (4, 3, 3, 2, 2, 1, 1)
CHIP_HOPS = (4, 3, 3, 3, 3, 2, 2, 2, 2, 2, 2, 1, 1, 1, 1)
FAR_YX = (5, 7, 3, 4, 1, 6, 2, 0)
NT = (((1,), (1,)), ((), ()))
TN = (((0,), (0,)), ((), ()))


def normed(values, axis):
    centred = values - jnp.mean(values, axis=axis, keepdims=True)
    variance = jnp.mean(centred * centred, axis=axis, keepdims=True)
    return centred * lax.rsqrt(variance + 1e-05)


def dot(a, b, dims=(((1,), (0,)), ((), ()))):
    return lax.dot_general(a, b, dims, preferred_element_type=F32)


def lane_of(rows):
    return lax.broadcasted_iota(jnp.int32, (rows, 128), 1)


def rows_of_a(tiles):
    lane = lane_of(tiles[0].shape[0])
    t0, t1, t2 = tiles
    pieces = [
        t0,
        pltpu.roll(jnp.where(lane < 64, t1, t0), 32, 1),
        pltpu.roll(jnp.where(lane < 32, t2, t1), 64, 1),
        pltpu.roll(t2, 96, 1),
    ]
    return [jnp.where(lane < B, piece, 0.0) for piece in pieces]


def rows_of_b(tile, tail, tail_at):
    lane = lane_of(tile.shape[0])
    fifth = jnp.where(lane < 32, pltpu.roll(tile, 32, 1), pltpu.roll(tail, (32 - tail_at) % 128, 1))
    return [jnp.where(lane < B, piece, 0.0) for piece in (tile, fifth)]


def source_plane(base, e, d):
    return (base + 8 - d + e * (2 * d + 1)) & 7


def row_of(base, z, yx, r):
    delta = (z - base + 8) & 7
    e = jnp.where((delta >= 1) & (delta <= 4), 1, 0)
    d = jnp.where(e == 1, delta - 1, (8 - delta) & 7)
    return jnp.where(r < 4, e * 128 + yx * 16 + d * 4 + r, 256 + e * 64 + yx * 8 + d * 2 + r - 4)


def row_at(base, row):
    in_a, late = row < 256, row - 256
    e = jnp.where(in_a, row // 128, late // 64)
    yx = jnp.where(in_a, row % 128 // 16, late % 64 // 8)
    d = jnp.where(in_a, row % 16 // 4, late % 8 // 2)
    r = jnp.where(in_a, row % 4, 4 + late % 2)
    return source_plane(base, e, d), yx, r


def picks_outgoing(core, base):
    row = lax.broadcasted_iota(jnp.int32, (XLO * 128, YX * ROWS), 0)
    col = lax.broadcasted_iota(jnp.int32, (XLO * 128, YX * ROWS), 1)
    x_lo, jr = row // 128, row % 128
    z, yx, r = 4 * x_lo + 2 * core + jr // 48, jr % 48 // A, jr % A
    return jnp.where((col == row_of(base, z, yx, r)) & (jr < B), 1.0, 0.0).astype(BF16)


def picks_incoming(core, base):
    row = lax.broadcasted_iota(jnp.int32, (YX * ROWS, 4 * 128), 0)
    col = lax.broadcasted_iota(jnp.int32, (YX * ROWS, 4 * 128), 1)
    z, yx, r = row_at(base, row)
    other = jnp.bitwise_xor((z // 2) % 2, core)
    source = (other * 2 + z // 4) * 128 + (z % 2) * 48 + yx * A + r
    return jnp.where(col == source, 1.0, 0.0).astype(BF16)


def reorder(base, base_of_other):
    row = lax.broadcasted_iota(jnp.int32, (YX * ROWS, YX * ROWS), 0)
    col = lax.broadcasted_iota(jnp.int32, (YX * ROWS, YX * ROWS), 1)
    return jnp.where(col == row_of(base_of_other, *row_at(base, row)), 1.0, 0.0).astype(BF16)


def kernel(
    pair_hbm, proj_hbm, gate_hbm, out_hbm, o_ref,
    z_ref, proj_ref, gate_ref, out_ref, wide,
    senda, recva, send2, recv2, send1, recv1, spread, sendpa, sendpb, recvpa, recvpb, sendq, recvq, gather, sendx, recvx,
    load, zs, zr, ps, pr, cs, cr, qs, qr, xs, xr,
):
    loads = [
        pltpu.make_async_copy(src, dst, load.at[i])
        for i, (src, dst) in enumerate(
            ((pair_hbm, z_ref), (proj_hbm, proj_ref), (gate_hbm, gate_ref), (out_hbm, out_ref))
        )
    ]
    loads[0].start()
    loads[1].start()
    row, col = lax.axis_index("row"), lax.axis_index("col")
    plane, yx, x_lo, core = row >> 3, row & 7, col >> 1, col & 1
    chip = yx * XLO + x_lo
    chunk_of_chip = x_lo ^ ((yx >> 1) & 1)
    member = (plane + 8 - core) & 1
    base, base_of_other = (plane + 8 - member) & 7, (plane + 7 + member) & 7
    up = 1 - 2 * member
    relays = [((plane + 8 + step * up) & 7, d) for d, step in ((3, -3), (2, 2), (1, -1))]
    planes = [(plane + s) & (Z - 1) for s in FAR_PLANES]
    chips = [chip ^ s for s in FAR_CHIPS]

    def on_plane(other_plane):
        return {"row": other_plane * YX + yx, "col": col}

    def on_chip(other_chip, of_plane=plane):
        return {"row": of_plane * YX + (other_chip >> 1), "col": (other_chip & 1) * CORES + core}

    other_core = {"row": row, "col": col ^ 1}

    barrier = pltpu.get_barrier_semaphore()
    beside = (plane + 8 + up) & 7
    peers = [(hops, on_plane(peer)) for hops, peer in zip(PLANE_HOPS, planes)]
    peers += [(hops, on_chip(peer)) for hops, peer in zip(CHIP_HOPS, chips)]
    peers += [(hops + 1, on_chip(peer, beside)) for hops, peer in zip(CHIP_HOPS, chips)]
    peers = [peer for _, peer in sorted(peers, key=lambda peer: -peer[0])] + [other_core]
    for peer in peers:
        pl.semaphore_signal(barrier, inc=1, device_id=peer, device_id_type=MESH)
    loads[2].start()
    loads[3].start()

    sent = []

    def remote(src, dst, send, recv, peer):
        pltpu.make_async_remote_copy(
            src_ref=src, dst_ref=dst, send_sem=send, recv_sem=recv, device_id=peer, device_id_type=MESH
        ).start()

    def arrived(ref, sem):
        pltpu.make_async_copy(ref, ref, sem).wait()

    def slot_of(some_chip):
        return (some_chip & 1) * YX + (some_chip >> 1)

    def over_planes(src, dst, send, recv):
        for peer in planes:
            remote(src.at[peer], dst.at[plane], send, recv, on_plane(peer))
        pltpu.make_async_copy(src.at[plane], dst.at[plane], recv).start()
        sent.append((src.at[pl.ds(0, Z - 1)], send))

    def to_owners(chunk, src, dst, send, recv):
        here = dst.at[member * CHIPS + slot_of(chip)]

        def owner(m):
            return m * XLO + (chunk ^ ((m >> 1) & 1))

        for s in FAR_YX:
            peer = yx ^ s
            remote(src.at[1 - member, peer], here, send, recv, on_chip(owner(peer), beside))
            if s != 0:
                remote(src.at[member, peer], here, send, recv, on_chip(owner(peer)))
        own = chunk_of_chip == chunk

        @pl.when(own)
        def _():
            pltpu.make_async_copy(src.at[member, yx], here, recv).start()

        @pl.when(jnp.logical_not(own))
        def _():
            remote(src.at[member, yx], here, send, recv, on_chip(chip ^ 1))

    def wide_weights(u):
        for i in range(4):
            turned = proj_ref[u, i].astype(F32).T.reshape(Z, 2, HALF, C)
            for k in range(2):
                wide[u, k, i] = turned[:, k].reshape(Z * HALF, C).astype(BF16)

    def drain(count):
        for _ in range(count):
            arrived(*sent.pop(0))

    def z_parts(u):
        return [
            (senda.at[u, 0], recva.at[u, 0]),
            (send2.at[u], recv2.at[u]),
            (senda.at[u, 1], recva.at[u, 1]),
            (send1.at[u], recv1.at[u]),
        ]

    def issue(u, i):
        src, dst = z_parts(u)[i]
        for relay, d in relays:
            first = (relay + 8 - (member ^ (d & 1))) & 7
            for e in range(2):
                remote(src.at[(first + e) & 7], dst.at[2 * d + e], zs.at[u, i], zr.at[u, i], on_plane(relay))
        for e in range(2):
            pltpu.make_async_copy(src.at[(base + e) & 7], dst.at[e], zr.at[u, i]).start()
        sent.append((src.at[pl.ds(0, 6)], zs.at[u, i]))

    def edges(u, k, zn):
        both = dot(wide[u, k].reshape(4 * Z * HALF, C), zn, NT).reshape(4, Z, HALF, zn.shape[0])
        left = jax.nn.sigmoid(both[0]) * both[1]
        right = jax.nn.sigmoid(both[2]) * both[3]
        return jnp.concatenate([left, right], axis=1).astype(BF16)

    def head_a(u, rows):
        zn = normed(rows.reshape(4 * B, C), -1).astype(BF16)
        senda[u, 0] = edges(u, 0, zn)
        if u == 1:
            issue(u, 0)
        return zn

    def head_b(u, zn_a, rows):
        zn = normed(rows.reshape(2 * B, C), -1).astype(BF16)
        second = edges(u, 1, zn)
        send2[u, :, :, 0:192] = edges(u, 0, zn)
        send2[u, :, :, 192:256] = second[:, :, 128:192]
        send1[u] = second[:, :, 0:128]
        if u == 1:
            issue(u, 1)
        senda[u, 1] = edges(u, 1, zn_a)
        if u == 0:
            pl.semaphore_wait(barrier, len(peers))
            issue(u, 0)
            issue(u, 1)
        issue(u, 2)
        issue(u, 3)
        return zn

    def body(u, zn, before):
        if u == 0:
            wide_weights(1)
            loads[2].wait()
            loads[3].wait()
        gate = [jax.nn.sigmoid(dot(some, gate_ref[u])) for some in zn]
        picks = picks_outgoing(core, base) if u == 0 else picks_incoming(core, base)
        other_picks = picks_outgoing(core, base_of_other) if u == 0 else None
        in_order = reorder(base, base_of_other)
        drain(before)

        for k in range(2):
            for part in range(2):
                arrived(z_parts(u)[2 * k + part][1], zr.at[u, 2 * k + part])

                def spread_plane(p, carry):
                    if part == 0:
                        tiles = [recva[u, k, p, :, t * 128 : t * 128 + 128].astype(F32) for t in range(3)]
                        pieces = rows_of_a(tiles)
                    else:
                        tile = recv2[u, p, :, 0:128] if k == 0 else recv1[u, p]
                        pieces = rows_of_b(tile.astype(F32), recv2[u, p, :, 128:256].astype(F32), 64 * k)
                    d, e = p >> 1, p & 1
                    for i, piece in enumerate(pieces):
                        at = e * 2 * HALF * 24 + (d * 4 + i if part == 0 else 16 + d * 2 + i)
                        spread[u, k, pl.ds(at, 2 * HALF, stride=24), :] = piece
                    return carry

                lax.fori_loop(0, Z, spread_plane, 0, unroll=True)
                for e in range(2):
                    for m in range(HALF):
                        at = [(e * 2 * HALF + side * HALF + m) * 24 for side in range(2)]
                        if part == 0:
                            for side in range(2):
                                sendpa[u, k, e, m, side] = spread[u, k, at[side] : at[side] + 16, :].astype(BF16)
                        else:
                            both = [spread[u, k, at[side] + 16 : at[side] + 24, :] for side in range(2)]
                            sendpb[u, k, e, m] = jnp.concatenate(both, axis=0).astype(BF16)
                sendp, recvp = ((sendpa, recvpa), (sendpb, recvpb))[part]
                to_owners(k, sendp.at[u, k], recvp.at[u, 0], ps.at[u, part], pr.at[u, part])

        def shared(part, c):
            if u == 1 and part == 0:
                return recvpa.at[u, c, :, 0]
            return (recvpa, recvpb)[part].at[u, c]

        for part, recvp in enumerate((recvpa, recvpb)):
            sent.append((recvp.at[u, 0, pl.ds(0, 2 * CHIPS - 1)], ps.at[u, part]))
            arrived(recvp.at[u, 0], pr.at[u, part])
            remote(shared(part, 0), shared(part, 1), cs.at[u, part], cr.at[u, part], other_core)
            sent.append((shared(part, 0), cs.at[u, part]))

        def block_of(part, side, c, x):
            rows = []
            for e in range(2):
                slots = pl.ds(e * CHIPS + x * YX, YX)
                if part == 0:
                    rows.append(recvpa[u, c, slots, side].reshape(128, 128))
                else:
                    both = recvpb[u, c, slots].astype(F32)
                    rows.append(both[:, side * 8 : side * 8 + 8].reshape(64, 128).astype(BF16))
            return jnp.concatenate(rows, axis=0)

        def blocks(part, side, c):
            return jnp.concatenate([block_of(part, side, c, x) for x in range(XLO)], axis=1)

        halves, lefts = [], []
        for part in range(2):
            arrived(shared(part, 1), cr.at[u, part])
            here = slice(256 * part, 256 + 128 * part)
            left_of_other = dot(in_order[here, here], blocks(part, 0, 1)).astype(BF16)
            left = jnp.concatenate([blocks(part, 0, 0), left_of_other], axis=1)
            if u == 0:
                right = [dot(which[:, here], blocks(part, 1, c)) for c, which in enumerate((picks, other_picks))]
                halves.append(jnp.concatenate(right, axis=1))
                lefts.append(left)
            else:
                halves.append(dot(dot(picks, left, NT).astype(BF16), blocks(part, 1, 0)))
        tri = halves[0] + halves[1]
        if u == 0:
            tri = dot(jnp.concatenate(lefts, axis=0), tri.astype(BF16), NT)
        for x in range(XLO):
            block = tri[:, x * 128 : x * 128 + 128]
            slots = pl.ds(x * YX, YX)
            for e in range(2):
                part_a = block[e * 128 : e * 128 + 128].astype(BF16)
                sendq[u, slots, e * 16 : e * 16 + 16] = part_a.reshape(YX, 16, 128)
            part_b = block[256:384].reshape(2, YX, 8, 128)
            sendq[u, slots, 32:48] = jnp.concatenate([part_b[0], part_b[1]], axis=1).astype(BF16)
        here = recvq.at[u, chunk_of_chip, yx]
        for peer in chips:
            remote(sendq.at[u, slot_of(peer)], here, qs.at[u], qr.at[u, chunk_of_chip], on_chip(peer))
        pltpu.make_async_copy(sendq.at[u, slot_of(chip)], here, qr.at[u, chunk_of_chip]).start()
        sent.append((sendq.at[u, pl.ds(0, CHIPS - 1)], qs.at[u]))

        if u == 1:
            drain(len(sent))
        for k in range(2):
            arrived(recvq.at[u, k], qr.at[u, k])
            gather[u, k] = recvq[u, k].reshape(HALF * ROWS, 128).astype(F32)

            def gather_plane(p, carry):
                d, e = p >> 1, p & 1
                for r in range(0, A, 2):
                    at = e * 16 + d * 4 + r if r < 4 else 32 + e * 8 + d * 2
                    pair_of_rows = [gather[u, k, pl.ds(at + i, HALF, stride=ROWS), :] for i in range(2)]
                    tile = jnp.concatenate(pair_of_rows, axis=0).astype(BF16)
                    sendx[u, k, source_plane(base, e, d), r * HALF : r * HALF + 2 * HALF] = tile
                return carry

            lax.fori_loop(0, Z, gather_plane, 0, unroll=True)
            over_planes(sendx.at[u, k], recvx.at[u, k], xs.at[u, k], xr.at[u, k])
        for k in range(2):
            arrived(recvx.at[u, k], xr.at[u, k])
        return gate

    def ending(u, pair, gate, first):
        tri = [recvx[u, k, p].astype(F32) for p in range(Z) for k in range(2)]
        for r in range(pair.shape[0]):
            at = (first + r) * HALF
            tri_row = jnp.concatenate([part[at : at + HALF] for part in tri], axis=0)
            projected = dot(normed(tri_row, 0).astype(BF16), out_ref[u], TN)[:B]
            o_ref[first + r] = pair[r] + gate[r * B : r * B + B] * projected

    loads[1].wait()
    wide_weights(0)
    loads[0].wait()
    zn_a = head_a(0, z_ref[0:4])
    zn_b = head_b(0, zn_a, z_ref[4:6])
    gate_a, gate_b = body(0, (zn_a, zn_b), 0)
    ending(0, z_ref[0:4], gate_a, 0)
    before = len(sent)
    zn_a = head_a(1, o_ref[0:4])
    ending(0, z_ref[4:6], gate_b, 4)
    zn_b = head_b(1, zn_a, o_ref[4:6])
    gate_a, gate_b = body(1, (zn_a, zn_b), before)
    ending(1, o_ref[0:4], gate_a, 0)
    ending(1, o_ref[4:6], gate_b, 4)
    drain(len(sent))


def solution(mesh):
    vmem = pl.BlockSpec(memory_space=pltpu.VMEM)

    def per_device(*operands):
        pair_rep, proj_weights, gate_weights, out_weights = operands
        return pl.pallas_call(
            kernel,
            out_shape=jax.ShapeDtypeStruct(pair_rep.shape, pair_rep.dtype),
            in_specs=[pl.BlockSpec(memory_space=pltpu.HBM)] * 4,
            out_specs=vmem,
            scratch_shapes=[
                pltpu.VMEM(pair_rep.shape, F32),
                pltpu.VMEM(proj_weights.shape, BF16),
                pltpu.VMEM(gate_weights.shape, BF16),
                pltpu.VMEM(out_weights.shape, BF16),
                pltpu.VMEM((2, 2, 4, Z * HALF, C), BF16),
                pltpu.VMEM((2, 2, Z, 2 * HALF, 384), BF16),
                pltpu.VMEM((2, 2, Z, 2 * HALF, 384), BF16),
                pltpu.VMEM((2, Z, 2 * HALF, 256), BF16),
                pltpu.VMEM((2, Z, 2 * HALF, 256), BF16),
                pltpu.VMEM((2, Z, 2 * HALF, 128), BF16),
                pltpu.VMEM((2, Z, 2 * HALF, 128), BF16),
                pltpu.VMEM((2, 2, 2 * HALF * ROWS, 128), F32),
                pltpu.VMEM((2, 2, 2, HALF, 2, 16, 128), BF16),
                pltpu.VMEM((2, 2, 2, HALF, 16, 128), BF16),
                pltpu.VMEM((2, CORES, 2 * CHIPS, 2, 16, 128), BF16),
                pltpu.VMEM((2, CORES, 2 * CHIPS, 16, 128), BF16),
                pltpu.VMEM((2, CHIPS, ROWS, 128), BF16),
                pltpu.VMEM((2, 2, HALF, ROWS, 128), BF16),
                pltpu.VMEM((2, 2, HALF * ROWS, 128), F32),
                pltpu.VMEM((2, 2, Z, A * HALF, 128), BF16),
                pltpu.VMEM((2, 2, Z, A * HALF, 128), BF16),
                pltpu.SemaphoreType.DMA((4,)),
                pltpu.SemaphoreType.DMA((2, 4)),
                pltpu.SemaphoreType.DMA((2, 4)),
                pltpu.SemaphoreType.DMA((2, 2)),
                pltpu.SemaphoreType.DMA((2, 2)),
                pltpu.SemaphoreType.DMA((2, 2)),
                pltpu.SemaphoreType.DMA((2, 2)),
                pltpu.SemaphoreType.DMA((2,)),
                pltpu.SemaphoreType.DMA((2, 2)),
                pltpu.SemaphoreType.DMA((2, 2)),
                pltpu.SemaphoreType.DMA((2, 2)),
            ],
            compiler_params=pltpu.CompilerParams(
                collective_id=0, has_side_effects=True, vmem_limit_bytes=48 * 1024 * 1024
            ),
        )(*(pltpu.with_memory_space_constraint(x, pltpu.HBM) for x in operands))

    return jax.shard_map(
        per_device,
        mesh=mesh,
        in_specs=(P("row", "col", None), P(), P(), P()),
        out_specs=P("row", "col", None),
        check_vma=False,
    )
```

time: 64.4 us -> 63.5 us (0.986)
  Pallas kernels: 63.6 us -> 62.7 us
    pallas_call x1, Pallas kernels: 63.6 us -> 62.7 us  [per_device(): pl.pallas_call(kernel, out_shape=jax.ShapeDtypeStruct(pair_rep.shape, pai...]
where the time goes in v5:
time: 63.5 us
  Pallas kernels  62.7 us (99%)
  local copies, waits for them, and re-layouts  0.72 us (1%)
    pallas_call x1, Pallas kernels, per_device(): pl.pallas_call(kernel, out_shape=jax.ShapeDtypeStruct(pair_rep.shape, pai...  62.7 us

profile of v5, /device:TPU:1, one launch (start us, length us, event | category | flops | bytes accessed | tf_op | source)
XLA Modules:
  0.0 63.5 jit_solution(3509833166389283429)
XLA Ops:
  0.0 62.7 %shard_map.46 = f32[6,96,128]{2,1,0:T(8,128)S(1)} custom-call(f32[6,96,128]{2,1,0:T(8,128)} %pair_hbm.1, bf16[2,4,128,128]{3,2,1,0:T(8,128)(2,1)} %proj_hbm.1, bf16[2,128,128]{2,1,0:T(8,128)(2,1)} %gate_hbm.1, bf16[2,128,128]{2,1,0:T(8,128)(2,1)} %out_hbm.1), custom_call_target="tpu_custom_call" | custom-call | tf_op jit(solution)/shard_map/pallas_call | solution.py:387
  62.7 0.7 %copy.6 = f32[6,96,128]{2,1,0:T(8,128)} copy(f32[6,96,128]{2,1,0:T(8,128)S(1)} %shard_map.46) | data formatting | bytes 589824

commit v6 on v5

--- a/solution.py
+++ b/solution.py
@@ -337,7 +337,7 @@
             drain(len(sent))
         for k in range(2):
             arrived(recvq.at[u, k], qr.at[u, k])
-            gather[u, k] = recvq[u, k].reshape(HALF * ROWS, 128).astype(F32)
+            gather[u, k, 0 : HALF * ROWS] = recvq[u, k].reshape(HALF * ROWS, 128).astype(F32)
 
             def gather_plane(p, carry):
                 d, e = p >> 1, p & 1
@@ -401,14 +401,14 @@
                 pltpu.VMEM((2, Z, 2 * HALF, 256), BF16),
                 pltpu.VMEM((2, Z, 2 * HALF, 128), BF16),
                 pltpu.VMEM((2, Z, 2 * HALF, 128), BF16),
-                pltpu.VMEM((2, 2, 2 * HALF * ROWS, 128), F32),
+                pltpu.VMEM((2, 2, 2 * HALF * ROWS + 24, 128), F32),
                 pltpu.VMEM((2, 2, 2, HALF, 2, 16, 128), BF16),
                 pltpu.VMEM((2, 2, 2, HALF, 16, 128), BF16),
                 pltpu.VMEM((2, CORES, 2 * CHIPS, 2, 16, 128), BF16),
                 pltpu.VMEM((2, CORES, 2 * CHIPS, 16, 128), BF16),
                 pltpu.VMEM((2, CHIPS, ROWS, 128), BF16),
                 pltpu.VMEM((2, 2, HALF, ROWS, 128), BF16),
-                pltpu.VMEM((2, 2, HALF * ROWS, 128), F32),
+                pltpu.VMEM((2, 2, HALF * ROWS + ROWS, 128), F32),
                 pltpu.VMEM((2, 2, Z, A * HALF, 128), BF16),
                 pltpu.VMEM((2, 2, Z, A * HALF, 128), BF16),
                 pltpu.SemaphoreType.DMA((4,)),

time: 63.5 us -> 63.5 us (level)
  no operation moved by 1% of the time
where the time goes in v6:
time: 63.5 us
  Pallas kernels  62.7 us (99%)
  local copies, waits for them, and re-layouts  0.72 us (1%)
    pallas_call x1, Pallas kernels, per_device(): pl.pallas_call(kernel, out_shape=jax.ShapeDtypeStruct(pair_rep.shape, pai...  62.7 us

profile of v6, /device:TPU:1, one launch (start us, length us, event | category | flops | bytes accessed | tf_op | source)
XLA Modules:
  0.0 63.5 jit_solution(4768651414668665449)
XLA Ops:
  0.0 62.7 %shard_map.46 = f32[6,96,128]{2,1,0:T(8,128)S(1)} custom-call(f32[6,96,128]{2,1,0:T(8,128)} %pair_hbm.1, bf16[2,4,128,128]{3,2,1,0:T(8,128)(2,1)} %proj_hbm.1, bf16[2,128,128]{2,1,0:T(8,128)(2,1)} %gate_hbm.1, bf16[2,128,128]{2,1,0:T(8,128)(2,1)} %out_hbm.1), custom_call_target="tpu_custom_call" | custom-call | tf_op jit(solution)/shard_map/pallas_call | solution.py:387
  62.7 0.7 %copy.6 = f32[6,96,128]{2,1,0:T(8,128)} copy(f32[6,96,128]{2,1,0:T(8,128)S(1)} %shard_map.46) | data formatting | bytes 589824

commit v7 on v6

--- a/solution.py
+++ b/solution.py
@@ -327,6 +327,7 @@
                 sendq[u, slots, e * 16 : e * 16 + 16] = part_a.reshape(YX, 16, 128)
             part_b = block[256:384].reshape(2, YX, 8, 128)
             sendq[u, slots, 32:48] = jnp.concatenate([part_b[0], part_b[1]], axis=1).astype(BF16)
+        drain(len(sent))
         here = recvq.at[u, chunk_of_chip, yx]
         for peer in chips:
             remote(sendq.at[u, slot_of(peer)], here, qs.at[u], qr.at[u, chunk_of_chip], on_chip(peer))

time: 63.5 us -> 63.7 us (level)
  no operation moved by 1% of the time
where the time goes in v7:
time: 63.7 us; the launch traced here: 63.6 us
  Pallas kernels  62.9 us (99%)
  local copies, waits for them, and re-layouts  0.72 us (1%)
    pallas_call x1, Pallas kernels, per_device(): pl.pallas_call(kernel, out_shape=jax.ShapeDtypeStruct(pair_rep.shape, pai...  62.9 us

profile of v7, /device:TPU:1, one launch (start us, length us, event | category | flops | bytes accessed | tf_op | source)
XLA Modules:
  0.0 63.6 jit_solution(3728580991361791689)
XLA Ops:
  0.0 62.9 %shard_map.46 = f32[6,96,128]{2,1,0:T(8,128)S(1)} custom-call(f32[6,96,128]{2,1,0:T(8,128)} %pair_hbm.1, bf16[2,4,128,128]{3,2,1,0:T(8,128)(2,1)} %proj_hbm.1, bf16[2,128,128]{2,1,0:T(8,128)(2,1)} %gate_hbm.1, bf16[2,128,128]{2,1,0:T(8,128)(2,1)} %out_hbm.1), custom_call_target="tpu_custom_call" | custom-call | tf_op jit(solution)/shard_map/pallas_call | solution.py:388
  62.9 0.7 %copy.6 = f32[6,96,128]{2,1,0:T(8,128)} copy(f32[6,96,128]{2,1,0:T(8,128)S(1)} %shard_map.46) | data formatting | bytes 589824

commit v8 on v6

--- a/solution.py
+++ b/solution.py
@@ -99,7 +99,7 @@
 def kernel(
     pair_hbm, proj_hbm, gate_hbm, out_hbm, o_ref,
     z_ref, proj_ref, gate_ref, out_ref, wide,
-    senda, recva, send2, recv2, send1, recv1, spread, sendpa, sendpb, recvpa, recvpb, sendq, recvq, gather, sendx, recvx,
+    senda, recva, send2, recv2, send1, recv1, spread, sendpa, sendpb, recvpa, recvpb, sendq, recvq, gather, sendx, recvx, sendy, recvy,
     load, zs, zr, ps, pr, cs, cr, qs, qr, xs, xr,
 ):
     loads = [
@@ -341,26 +341,45 @@
 
             def gather_plane(p, carry):
                 d, e = p >> 1, p & 1
-                for r in range(0, A, 2):
-                    at = e * 16 + d * 4 + r if r < 4 else 32 + e * 8 + d * 2
-                    pair_of_rows = [gather[u, k, pl.ds(at + i, HALF, stride=ROWS), :] for i in range(2)]
-                    tile = jnp.concatenate(pair_of_rows, axis=0).astype(BF16)
-                    sendx[u, k, source_plane(base, e, d), r * HALF : r * HALF + 2 * HALF] = tile
+                lane = lane_of(2 * HALF)
+                threes = []
+                for i in range(3):
+                    rows = []
+                    for r in (i, 3 + i):
+                        at = e * 16 + d * 4 + r if r < 4 else 32 + e * 8 + d * 2 + r - 4
+                        rows.append(gather[u, k, pl.ds(at, HALF, stride=ROWS), :])
+                    threes.append(jnp.concatenate(rows, axis=0))
+                t0, t1, t2 = threes[0], pltpu.roll(threes[1], 96, 1), pltpu.roll(threes[2], 64, 1)
+                to = source_plane(base, e, d)
+                tiles = [jnp.where(lane < 96, t0, t1), jnp.where(lane < 64, t1, t2)]
+                for t, tile in enumerate(tiles):
+                    (sendx, sendy)[k][u, to, :, t * 128 : t * 128 + 128] = tile.astype(BF16)
+                if k == 0:
+                    sendy[u, to, :, 256:384] = pltpu.roll(t2, 32, 1).astype(BF16)
+                else:
+                    kept = sendy[u, to, :, 256:384].astype(F32)
+                    sendy[u, to, :, 256:384] = jnp.where(lane < 32, t2, kept).astype(BF16)
                 return carry
 
             lax.fori_loop(0, Z, gather_plane, 0, unroll=True)
-            over_planes(sendx.at[u, k], recvx.at[u, k], xs.at[u, k], xr.at[u, k])
+            over_planes((sendx, sendy)[k].at[u], (recvx, recvy)[k].at[u], xs.at[u, k], xr.at[u, k])
         for k in range(2):
-            arrived(recvx.at[u, k], xr.at[u, k])
+            arrived((recvx, recvy)[k].at[u], xr.at[u, k])
         return gate
 
-    def ending(u, pair, gate, first):
-        tri = [recvx[u, k, p].astype(F32) for p in range(Z) for k in range(2)]
-        for r in range(pair.shape[0]):
-            at = (first + r) * HALF
-            tri_row = jnp.concatenate([part[at : at + HALF] for part in tri], axis=0)
-            projected = dot(normed(tri_row, 0).astype(BF16), out_ref[u], TN)[:B]
-            o_ref[first + r] = pair[r] + gate[r * B : r * B + B] * projected
+    def ending(u, pair, gate):
+        gate = jnp.concatenate(gate, axis=0)
+        for h in range(2):
+            parts = []
+            for p in range(Z):
+                first = recvx[u, p].astype(F32)[h * HALF : h * HALF + HALF]
+                second = recvy[u, p].astype(F32)[h * HALF : h * HALF + HALF]
+                parts.append(jnp.concatenate([first, pltpu.roll(second[:, 256:384], 96, 1)], axis=1))
+                parts.append(second)
+            tri = jnp.concatenate(parts, axis=0)
+            projected = dot(normed(tri, 0).astype(BF16), out_ref[u], TN)[: 3 * B]
+            here = slice(h * 3 * B, h * 3 * B + 3 * B)
+            o_ref[3 * h : 3 * h + 3] = pair[3 * h : 3 * h + 3] + (gate[here] * projected).reshape(3, B, C)
 
     loads[1].wait()
     wide_weights(0)
@@ -368,14 +387,12 @@
     zn_a = head_a(0, z_ref[0:4])
     zn_b = head_b(0, zn_a, z_ref[4:6])
     gate_a, gate_b = body(0, (zn_a, zn_b), 0)
-    ending(0, z_ref[0:4], gate_a, 0)
+    ending(0, z_ref, (gate_a, gate_b))
     before = len(sent)
     zn_a = head_a(1, o_ref[0:4])
-    ending(0, z_ref[4:6], gate_b, 4)
     zn_b = head_b(1, zn_a, o_ref[4:6])
     gate_a, gate_b = body(1, (zn_a, zn_b), before)
-    ending(1, o_ref[0:4], gate_a, 0)
-    ending(1, o_ref[4:6], gate_b, 4)
+    ending(1, o_ref, (gate_a, gate_b))
     drain(len(sent))
 
 
@@ -409,8 +426,10 @@
                 pltpu.VMEM((2, CHIPS, ROWS, 128), BF16),
                 pltpu.VMEM((2, 2, HALF, ROWS, 128), BF16),
                 pltpu.VMEM((2, 2, HALF * ROWS + ROWS, 128), F32),
-                pltpu.VMEM((2, 2, Z, A * HALF, 128), BF16),
-                pltpu.VMEM((2, 2, Z, A * HALF, 128), BF16),
+                pltpu.VMEM((2, Z, 2 * HALF, 256), BF16),
+                pltpu.VMEM((2, Z, 2 * HALF, 256), BF16),
+                pltpu.VMEM((2, Z, 2 * HALF, 384), BF16),
+                pltpu.VMEM((2, Z, 2 * HALF, 384), BF16),
                 pltpu.SemaphoreType.DMA((4,)),
                 pltpu.SemaphoreType.DMA((2, 4)),
                 pltpu.SemaphoreType.DMA((2, 4)),

time: 63.5 us -> 62.7 us (0.987)
  Pallas kernels: 62.7 us -> 61.9 us
    pallas_call x1, Pallas kernels: 62.7 us -> 61.9 us  [per_device(): pl.pallas_call(kernel, out_shape=jax.ShapeDtypeStruct(pair_rep.shape, pai...]
where the time goes in v8:
time: 62.7 us; the launch traced here: 62.6 us
  Pallas kernels  61.9 us (99%)
  local copies, waits for them, and re-layouts  0.72 us (1%)
    pallas_call x1, Pallas kernels, per_device(): pl.pallas_call(kernel, out_shape=jax.ShapeDtypeStruct(pair_rep.shape, pai...  61.9 us

profile of v8, /device:TPU:1, one launch (start us, length us, event | category | flops | bytes accessed | tf_op | source)
XLA Modules:
  0.0 62.6 jit_solution(16042017581063072508)
XLA Ops:
  0.0 61.9 %shard_map.46 = f32[6,96,128]{2,1,0:T(8,128)S(1)} custom-call(f32[6,96,128]{2,1,0:T(8,128)} %pair_hbm.1, bf16[2,4,128,128]{3,2,1,0:T(8,128)(2,1)} %proj_hbm.1, bf16[2,128,128]{2,1,0:T(8,128)(2,1)} %gate_hbm.1, bf16[2,128,128]{2,1,0:T(8,128)(2,1)} %out_hbm.1), custom_call_target="tpu_custom_call" | custom-call | tf_op jit(solution)/shard_map/pallas_call | solution.py:404
  61.9 0.7 %copy.6 = f32[6,96,128]{2,1,0:T(8,128)} copy(f32[6,96,128]{2,1,0:T(8,128)S(1)} %shard_map.46) | data formatting | bytes 589824

commit v9 on v8

--- a/solution.py
+++ b/solution.py
@@ -198,15 +198,18 @@
             (send1.at[u], recv1.at[u]),
         ]
 
-    def issue(u, i):
+    def issue(u, i, lanes=None, last=True):
         src, dst = z_parts(u)[i]
+        if lanes is not None:
+            src, dst = src.at[:, :, lanes], dst.at[:, :, lanes]
         for relay, d in relays:
             first = (relay + 8 - (member ^ (d & 1))) & 7
             for e in range(2):
                 remote(src.at[(first + e) & 7], dst.at[2 * d + e], zs.at[u, i], zr.at[u, i], on_plane(relay))
         for e in range(2):
             pltpu.make_async_copy(src.at[(base + e) & 7], dst.at[e], zr.at[u, i]).start()
-        sent.append((src.at[pl.ds(0, 6)], zs.at[u, i]))
+        if last:
+            sent.append((z_parts(u)[i][0].at[pl.ds(0, 6)], zs.at[u, i]))
 
     def edges(u, k, zn):
         both = dot(wide[u, k].reshape(4 * Z * HALF, C), zn, NT).reshape(4, Z, HALF, zn.shape[0])
@@ -367,9 +370,9 @@
             arrived((recvx, recvy)[k].at[u], xr.at[u, k])
         return gate
 
-    def ending(u, pair, gate):
+    def ending(u, pair, gate, halves=(0, 1)):
         gate = jnp.concatenate(gate, axis=0)
-        for h in range(2):
+        for h in halves:
             parts = []
             for p in range(Z):
                 first = recvx[u, p].astype(F32)[h * HALF : h * HALF + HALF]
@@ -387,9 +390,16 @@
     zn_a = head_a(0, z_ref[0:4])
     zn_b = head_b(0, zn_a, z_ref[4:6])
     gate_a, gate_b = body(0, (zn_a, zn_b), 0)
-    ending(0, z_ref, (gate_a, gate_b))
+    ending(0, z_ref, (gate_a, gate_b), (0,))
     before = len(sent)
-    zn_a = head_a(1, o_ref[0:4])
+    zn = normed(o_ref[0:3].reshape(3 * B, C), -1).astype(BF16)
+    senda[1, 0, :, :, 0:256] = edges(1, 0, zn[0:256])
+    issue(1, 0, pl.ds(0, 256), False)
+    ending(0, z_ref, (gate_a, gate_b), (1,))
+    late = normed(o_ref[3].reshape(B, C), -1).astype(BF16)
+    zn_a = jnp.concatenate([zn, late], axis=0)
+    senda[1, 0, :, :, 256:384] = edges(1, 0, zn_a[256:384])
+    issue(1, 0, pl.ds(256, 128))
     zn_b = head_b(1, zn_a, o_ref[4:6])
     gate_a, gate_b = body(1, (zn_a, zn_b), before)
     ending(1, o_ref, (gate_a, gate_b))

time: 62.7 us -> 63.3 us (level)
  no operation moved by 1% of the time
where the time goes in v9:
time: 63.3 us; the launch traced here: 63.2 us
  Pallas kernels  62.5 us (99%)
  local copies, waits for them, and re-layouts  0.72 us (1%)
    pallas_call x1, Pallas kernels, per_device(): pl.pallas_call(kernel, out_shape=jax.ShapeDtypeStruct(pair_rep.shape, pai...  62.5 us

profile of v9, /device:TPU:1, one launch (start us, length us, event | category | flops | bytes accessed | tf_op | source)
XLA Modules:
  0.0 63.2 jit_solution(11292604941215920847)
XLA Ops:
  0.0 62.5 %shard_map.46 = f32[6,96,128]{2,1,0:T(8,128)S(1)} custom-call(f32[6,96,128]{2,1,0:T(8,128)} %pair_hbm.1, bf16[2,4,128,128]{3,2,1,0:T(8,128)(2,1)} %proj_hbm.1, bf16[2,128,128]{2,1,0:T(8,128)(2,1)} %gate_hbm.1, bf16[2,128,128]{2,1,0:T(8,128)(2,1)} %out_hbm.1), custom_call_target="tpu_custom_call" | custom-call | tf_op jit(solution)/shard_map/pallas_call | solution.py:414
  62.5 0.7 %copy.6 = f32[6,96,128]{2,1,0:T(8,128)} copy(f32[6,96,128]{2,1,0:T(8,128)S(1)} %shard_map.46) | data formatting | bytes 589824
